TPU v7x, 32 devices: a whole 2x2x4 slice. The times are simulated.
32 devices in a mesh: src: 4 (over x, core), tgt: 8 (over z, y).
Axes of the slice: x: 2, y: 2, z: 4, core: 2. Of those that a mesh axis runs over, the one named last changes fastest.
Arguments:
- src_feats: bfloat16 [32, 2560], P(None, ('src', 'tgt')), may hold values from -7 to 7
- src_factor: bfloat16 [16, 2560], P(None, ('src', 'tgt')), may hold values from 0.1 to 8
- tgt_feats: bfloat16 [32, 4096], P(None, ('tgt', 'src')), may hold values from -7 to 7
- tgt_factor: bfloat16 [16, 4096], P(None, ('tgt', 'src')), may hold values from 0.1 to 8
- rank_weight: float32 [16], replicated, may hold values from 0.5 to 4
Outputs:
- grad_src_feats: float32 [32, 2560], P(None, ('src', 'tgt'))
- grad_src_factor: float32 [16, 2560], P(None, ('src', 'tgt'))
- grad_tgt_feats: float32 [32, 4096], P(None, ('tgt', 'src'))
- grad_tgt_factor: float32 [16, 4096], P(None, ('tgt', 'src'))
All inputs are finite; a program needn't handle non-finite values.
Results may differ from a plain program's by a relative error of at most 0.0015.
Values may be sent and summed in bfloat16 or wider, within the bound.
A program may use at most 64 MiB of HBM per device.

v0:
```python
import jax
import jax.numpy as jnp
from jax import lax
from jax.sharding import PartitionSpec as P


def tile_terms(src_x, src_q, tgt_y, scaled_r, inverse_g):
    sq_src = jnp.sum(jnp.square(src_x.astype(jnp.float32)), 0)
    sq_tgt = jnp.sum(jnp.square(tgt_y.astype(jnp.float32)), 0)
    inner_prod = jnp.dot(src_x.T, tgt_y, preferred_element_type=jnp.float32)
    distance = jnp.sqrt(sq_src[:, None] + sq_tgt[None, :] - 2.0 * inner_prod + 1.0)
    plan_tile = jnp.dot(src_q.T, scaled_r, preferred_element_type=jnp.float32)
    weight = (plan_tile / distance).astype(jnp.bfloat16)
    cost_bf = distance.astype(jnp.bfloat16)
    row_mass = jnp.sum(weight.astype(jnp.float32), 1)
    col_mass = jnp.sum(weight.astype(jnp.float32), 0)
    grad_x = src_x.astype(jnp.float32) * row_mass[None, :] - jnp.dot(
        tgt_y, weight.T, preferred_element_type=jnp.float32
    )
    grad_q = jnp.dot(scaled_r, cost_bf.T, preferred_element_type=jnp.float32)
    grad_y = tgt_y.astype(jnp.float32) * col_mass[None, :] - jnp.dot(
        src_x, weight, preferred_element_type=jnp.float32
    )
    grad_r = inverse_g[:, None] * jnp.dot(src_q, cost_bf, preferred_element_type=jnp.float32)
    return (jnp.concatenate([grad_x, grad_q], 0), jnp.concatenate([grad_y, grad_r], 0))


def block_size(count):
    for candidate in (512, 256, 128):
        if count % candidate == 0:
            return candidate
    return count


def local(src_feats, src_factor, tgt_feats, tgt_factor, rank_weight):
    feature_count = src_feats.shape[0]
    stacked_count = feature_count + src_factor.shape[0]
    inverse_g = 1.0 / rank_weight
    tgt_whole = lax.all_gather(
        jnp.concatenate([tgt_feats, tgt_factor], 0), "src", axis=1, tiled=True
    )
    tgt_points = tgt_whole[:feature_count]
    scaled_r = (tgt_whole[feature_count:].astype(jnp.float32) * inverse_g[:, None]).astype(
        jnp.bfloat16
    )
    col_count = tgt_points.shape[1]
    total_tgt = tgt_feats.shape[1] * lax.axis_size("src") * lax.axis_size("tgt")
    src_stack = jnp.concatenate([src_feats, src_factor], 0)
    src_whole = lax.all_gather(src_stack, "tgt", axis=1, tiled=True)
    row_count = src_whole.shape[1]
    block_rows = block_size(row_count)

    def advance(block_index, totals):
        src_acc, tgt_acc = totals
        offset = block_index * block_rows
        part = lax.dynamic_slice_in_dim(src_whole, offset, block_rows, 1)
        src_part, tgt_part = tile_terms(
            part[:feature_count], part[feature_count:], tgt_points, scaled_r, inverse_g
        )
        src_acc = lax.dynamic_update_slice_in_dim(src_acc, src_part, offset, 1)
        tgt_acc = tgt_acc + tgt_part
        return (src_acc, tgt_acc)

    src_start = jnp.zeros((stacked_count, row_count), jnp.float32)
    tgt_start = jnp.zeros((stacked_count, col_count), jnp.float32)
    src_terms, tgt_terms = lax.fori_loop(
        0, row_count // block_rows, advance, (src_start, tgt_start)
    )
    src_sum = lax.psum_scatter(src_terms, "tgt", scatter_dimension=1, tiled=True)
    tgt_sum = lax.psum_scatter(tgt_terms, "src", scatter_dimension=1, tiled=True)
    scale = 1.0 / total_tgt
    return (
        src_sum[:feature_count] * scale,
        src_sum[feature_count:] * scale,
        tgt_sum[:feature_count] * scale,
        tgt_sum[feature_count:] * scale,
    )


def solution(mesh):
    placed = (
        P(None, ("src", "tgt")),
        P(None, ("src", "tgt")),
        P(None, ("tgt", "src")),
        P(None, ("tgt", "src")),
        P(),
    )
    return jax.shard_map(
        local,
        mesh=mesh,
        in_specs=placed,
        out_specs=(
            P(None, ("src", "tgt")),
            P(None, ("src", "tgt")),
            P(None, ("tgt", "src")),
            P(None, ("tgt", "src")),
        ),
        check_vma=False,
    )
```

profile of v0, /device:TPU:0, one launch (start us, length us, event | category | flops | bytes accessed | tf_op | source)
XLA Modules:
  0.0 149.9 jit_solution(12437547274202845918)
XLA Ops:
  7.2 0.7 broadcast_divide_fusion
  7.9 0.7 pad_maximum_fusion
  8.6 6.1 %all_gather.7 = bf16[48,512]{1,0:T(8,128)(2,1)S(1)} all-gather(bf16[48,128]{1,0:T(8,128)(2,1)S(1)} %pad_maximum_fusion), channel_id=1, replica_groups=mesh['src'=4,'tgt'=8] {'src'}, dimensions={1}, use_global_device_ids=true | all-gather | bytes 61440 | tf_op jit(solution)/shard_map/all_gather | solution.py:39
  14.7 0.6 copy-done
  15.4 0.6 copy-done.3
  16.0 31.4 %all-gather = bf16[8,80,48]{1,2,0:T(8,128)(2,1)S(1)} all-gather(bf16[1,80,48]{1,2,0:T(8,128)(2,1)S(1)} %maximum_bitcast_fusion), channel_id=1, replica_groups=mesh['src'=4,'tgt'=8] {'tgt'}, dimensions={0}, use_global_device_ids=true | all-gather | bytes 69120 | tf_op jit(solution)/shard_map/all_gather | solution.py:49
  47.7 0.7 slice-done
  48.4 6.5 %while.16 = (s32[]{:T(128)}, f32[48,640]{1,0:T(8,128)S(1)}, f32[48,512]{1,0:T(8,128)S(1)}, bf16[48,640]{1,0:T(8,128)(2,1)S(1)}, bf16[16,512]{1,0:T(8,128)(2,1)S(...) while((s32[]{:T(128)}, f32[48,640]{1,0:T(8,128)S(1)}, ...), condition=%wide.region_5.0_spmd.clone, body=%wide.region_0.0_spmd.clone.sunk | while | flops 19804936 | bytes 2124517 | solution.py:66
  49.0 0.3 convert_reduce_fusion.3
  49.7 0.3 fusion.49
  50.3 0.4 convert_reduce_fusion.3
  51.6 0.4 convert_reduce_fusion.3
  52.9 0.4 convert_reduce_fusion.3
  53.7 0.3 fusion.49
  54.2 0.4 convert_reduce_fusion.3
  54.9 0.6 copy-done.1
  55.6 0.9 copy.11
  56.5 19.6 %reduce-scatter.5.cloned.1.call-done = f32[48,128]{1,0:T(8,128)} async-done(((f32[48,512]{1,0:T(8,128)}), f32[48,128]{1,0:T(8,128)}) %reduce-scatter.5.cloned.1.call-update) | async-done | bytes 24592 | tf_op jit(solution)/shard_map/reduce_scatter | solution.py:70
  76.2 1.3 slice_multiply_fusion.1
  77.5 1.3 slice_multiply_fusion
  78.8 62.0 %reduce-scatter.7.cloned.1.call-done = f32[80,48]{1,0:T(8,128)} async-done(((f32[640,48]{1,0:T(8,128)}), f32[80,48]{1,0:T(8,128)}) %reduce-scatter.7.cloned.1.call-update) | async-done | bytes 15376
  140.8 0.9 slice.43
  141.8 0.6 broadcast_multiply_fusion
  142.4 0.6 broadcast_multiply_fusion.1
  (65 shorter events, 4.5 us)
Async XLA Ops:
  7.2 0.7 copy-start.4
  7.2 69.0 %reduce-scatter.5.cloned.1.call-start = ((), (), s32[]{:S(2)}) async-start(), calls=%async_computation.2 | async-start | bytes 122880 | tf_op jit(solution)/shard_map/reduce_scatter | solution.py:70
  14.7 0.6 copy-start
  15.3 0.7 copy-start.3
  15.3 0.7 copy-start.5
  47.6 0.8 slice-start
  54.9 0.6 copy-start.1
  55.6 85.2 %reduce-scatter.7.cloned.1.call-start = ((), (), s32[]{:S(2)}) async-start(), calls=%async_computation.3 | async-start | bytes 368640
  140.8 0.9 copy-start.2
Sparse Core Ops, SparseCore 0:
  55.7 20.4 reduce-scatter.4
  79.4 61.2 reduce-scatter.6
where the time goes:
time: 150 us
  waiting for transfers between devices  81.6 us (54%)
  blocking collectives  37.5 us (25%)
  between operations  14.1 us (9%)
  matrix products  5.84 us (4%)
  other arithmetic  5.78 us (4%)
  local copies, waits for them, and re-layouts  4.7 us (3%)
    unnamed x3, waiting for transfers between devices  62 us
    all_gather x1, blocking collectives, local(): src_whole = lax.all_gather(src_stack, 'tgt', axis=1, tiled=True)  31.4 us
    reduce_scatter x1, waiting for transfers between devices, local(): lax.psum_scatter(tgt_terms, 'src', scatter_dimension=1, tiled=True)  19.6 us
    all_gather x1, blocking collectives, local(): lax.all_gather(jnp.concatenate([tgt_feats, tgt_factor], 0), 'src', axis=1...  6.12 us
    unnamed x16, local copies, waits for them, and re-layouts  3.01 us
  transfers between devices with their start and end apart: 2, of which 2 were waited for; matrix products, arithmetic and copies ran while one was open for 2% of the time, Pallas kernels for 0%

commit v1 on v0

v1 whole, which is shorter than its diff:
```python
import functools

import jax
import jax.numpy as jnp
from jax import lax
from jax.experimental import pallas as pl
from jax.experimental.pallas import tpu as pltpu
from jax.sharding import PartitionSpec as P

MESH = pl.DeviceIdType.MESH
NT = (((1,), (1,)), ((), ()))
AUG = 16


def each(low, high, body):
    if high - low <= 8:
        for i in range(low, high):
            body(i)
    else:
        lax.fori_loop(low, high, lambda i, c: (body(i), c)[1], 0)


def split3(value):
    high = value.astype(jnp.bfloat16).astype(jnp.float32)
    rest = value - high
    mid = rest.astype(jnp.bfloat16).astype(jnp.float32)
    return high, mid, rest - mid


def aug_rows(feats, first, ones_at, extra):
    wide = feats.astype(jnp.float32)
    norm = jnp.sum(wide * wide, axis=0, keepdims=True) + extra
    high, mid, low = split3(norm)
    shape = (AUG, feats.shape[1])
    row = lax.broadcasted_iota(jnp.int32, shape, 0)
    out = jnp.where((row >= ones_at) & (row < ones_at + 3), 1.0, 0.0)
    for k, part in enumerate((high, mid, low)):
        out = jnp.where(row == first + k, jnp.broadcast_to(part, shape), out)
    return out.astype(jnp.bfloat16)


def kernel(
    n_src, n_tgt, scale,
    x_hbm, q_hbm, y_hbm, r_hbm, g_hbm,
    gx_ref, gq_ref, gy_ref, gr_ref,
    x_in, q_in, y_in, r_in, g_in,
    a_slots, t_slots, dist_rhs, plan_rhs, t_rows, s_rows, col_acc,
    src_out, src_in, tgt_out, tgt_in,
    load_sem, a_send, a_recv, t_send, t_recv, so_send, so_recv, to_send, to_recv,
):
    f = x_in.shape[0]
    k = q_in.shape[0]
    head = f + AUG
    cols_dev = y_in.shape[1]
    me_s = lax.axis_index("src")
    me_t = lax.axis_index("tgt")

    def tgt_peer(d):
        return lax.rem(me_t + d, n_tgt)

    def src_peer(d):
        return lax.rem(me_s + d, n_src)

    loads = [
        pltpu.make_async_copy(src, dst, load_sem.at[i])
        for i, (src, dst) in enumerate(
            ((y_hbm, y_in), (r_hbm, r_in), (g_hbm, g_in), (x_hbm, x_in), (q_hbm, q_in))
        )
    ]
    for load in loads:
        load.start()

    barrier = pltpu.get_barrier_semaphore()

    def greet_tgt(d):
        pl.semaphore_signal(
            barrier, inc=1, device_id={"src": me_s, "tgt": tgt_peer(d)}, device_id_type=MESH
        )

    def greet_src(d):
        pl.semaphore_signal(
            barrier, inc=1, device_id={"src": src_peer(d), "tgt": me_t}, device_id_type=MESH
        )

    each(1, n_tgt, greet_tgt)
    each(1, n_src, greet_src)

    for load in loads:
        load.wait()

    inv_row = 1.0 / g_in[...]
    square = (k, k)
    diagonal = lax.broadcasted_iota(jnp.int32, square, 0) == lax.broadcasted_iota(
        jnp.int32, square, 1
    )
    inverse_g = jnp.sum(
        jnp.where(diagonal, jnp.broadcast_to(inv_row, square), 0.0), axis=1, keepdims=True
    )
    y = y_in[...]
    t_slots[me_s, 0:f, :] = y
    t_slots[me_s, f:head, :] = aug_rows(y, 3, 0, 1.0)
    t_slots[me_s, head:, :] = (r_in[...].astype(jnp.float32) * inverse_g).astype(jnp.bfloat16)
    x = x_in[...]
    a_slots[me_t, 0:f, :] = (x.astype(jnp.float32) * -2.0).astype(jnp.bfloat16)
    a_slots[me_t, f:head, :] = aug_rows(x, 0, 3, 0.0)
    a_slots[me_t, head:, :] = q_in[...]

    pl.semaphore_wait(barrier, n_tgt + n_src - 2)

    def t_copy(d, slot):
        return pltpu.make_async_remote_copy(
            src_ref=t_slots.at[slot], dst_ref=t_slots.at[slot],
            send_sem=t_send.at[d], recv_sem=t_recv.at[slot],
            device_id={"src": src_peer(d), "tgt": me_t}, device_id_type=MESH,
        )

    def a_copy(d, slot):
        return pltpu.make_async_remote_copy(
            src_ref=a_slots.at[slot], dst_ref=a_slots.at[slot],
            send_sem=a_send.at[d], recv_sem=a_recv.at[slot],
            device_id={"src": me_s, "tgt": tgt_peer(d)}, device_id_type=MESH,
        )

    each(1, n_src, lambda d: t_copy(d, me_s).start())
    each(1, n_tgt, lambda d: a_copy(d, me_t).start())

    each(1, n_src, lambda d: t_copy(d, src_peer(d)).wait_recv())
    for s in range(n_src):
        at = pl.ds(s * cols_dev, cols_dev)
        t_rows[:, at] = t_slots[s, 0:head, :]
        s_rows[:, at] = t_slots[s, head:, :]
        dist_rhs[0:head, at] = t_slots[s, 0:head, :]
        plan_rhs[head:, at] = t_slots[s, head:, :]
    dist_rhs[head:, :] = jnp.zeros((k, dist_rhs.shape[1]), jnp.bfloat16)
    plan_rhs[0:head, :] = jnp.zeros((head, plan_rhs.shape[1]), jnp.bfloat16)

    def so_copy(d, from_slot, to_slot):
        return pltpu.make_async_remote_copy(
            src_ref=src_out.at[from_slot], dst_ref=src_in.at[to_slot],
            send_sem=so_send.at[d], recv_sem=so_recv.at[to_slot],
            device_id={"src": me_s, "tgt": tgt_peer(d)}, device_id_type=MESH,
        )

    def block(d):
        peer = tgt_peer(d)
        static = isinstance(d, int)
        if not (static and d == 0):
            a_copy(d, peer).wait_recv()
        a = a_slots[peer]
        at = a.astype(jnp.float32).T.astype(jnp.bfloat16)
        squared = jnp.dot(at, dist_rhs[...], preferred_element_type=jnp.float32)
        plan = jnp.dot(at, plan_rhs[...], preferred_element_type=jnp.float32)
        inv = lax.rsqrt(squared)
        weight = (plan * inv).astype(jnp.bfloat16)
        cost = (squared * inv).astype(jnp.bfloat16)
        w_sum = lax.dot_general(t_rows[...], weight, NT, preferred_element_type=jnp.float32)
        c_sum = lax.dot_general(s_rows[...], cost, NT, preferred_element_type=jnp.float32)
        src_out[d, 0:f, :] = (
            a[0:f].astype(jnp.float32) * (-0.5 * w_sum[f : f + 1]) - w_sum[0:f]
        )
        src_out[d, f:, :] = c_sum
        if not (static and d == 0):
            so_copy(d, d, me_t).start()
        aw = jnp.dot(a[0:head], weight, preferred_element_type=jnp.float32)
        ac = jnp.dot(a[head:], cost, preferred_element_type=jnp.float32)
        if static and d == 0:
            col_acc[0:head, :] = aw
            col_acc[head:, :] = ac
        else:
            col_acc[0:head, :] += aw
            col_acc[head:, :] += ac

    block(0)
    each(1, n_tgt, block)

    def to_copy(d, from_slot, to_slot):
        return pltpu.make_async_remote_copy(
            src_ref=tgt_out.at[from_slot], dst_ref=tgt_in.at[to_slot],
            send_sem=to_send.at[d], recv_sem=to_recv.at[to_slot],
            device_id={"src": src_peer(d), "tgt": me_t}, device_id_type=MESH,
        )

    for s in range(n_src):
        at = pl.ds(s * cols_dev, cols_dev)
        mass = col_acc[f + 3 : f + 4, at]
        tgt_out[s, 0:f, :] = t_rows[0:f, at].astype(jnp.float32) * mass + 0.5 * col_acc[0:f, at]
        tgt_out[s, f:, :] = col_acc[head:, at]
    each(1, n_src, lambda d: to_copy(d, src_peer(d), me_s).start())

    total = [src_out[0]]

    def add_src(d):
        peer = tgt_peer(d)
        so_copy(d, d, peer).wait_recv()
        src_out[0] += src_in[peer]

    each(1, n_tgt, add_src)
    gx_ref[...] = src_out[0, 0:f, :] * scale
    gq_ref[...] = src_out[0, f:, :] * scale

    def add_tgt(d):
        peer = src_peer(d)
        to_copy(d, peer, peer).wait_recv()
        tgt_out[me_s] += tgt_in[peer]

    each(1, n_src, add_tgt)
    gy_ref[...] = tgt_out[me_s, 0:f, :] * scale
    gr_ref[...] = tgt_out[me_s, f:, :] * inverse_g * scale

    each(1, n_src, lambda d: t_copy(d, me_s).wait_send())
    each(1, n_tgt, lambda d: a_copy(d, me_t).wait_send())
    each(1, n_tgt, lambda d: so_copy(d, d, me_t).wait_send())
    each(1, n_src, lambda d: to_copy(d, src_peer(d), me_s).wait_send())


def local(src_feats, src_factor, tgt_feats, tgt_factor, rank_weight):
    n_src = lax.axis_size("src")
    n_tgt = lax.axis_size("tgt")
    f, rows = src_feats.shape
    k = src_factor.shape[0]
    cols = tgt_feats.shape[1]
    wide = n_src * cols
    stack = f + AUG + k
    f32, bf16 = jnp.float32, jnp.bfloat16
    scale = 1.0 / (cols * n_src * n_tgt)
    vmem = pl.BlockSpec(memory_space=pltpu.VMEM)
    dma = pltpu.SemaphoreType.DMA
    return pl.pallas_call(
        functools.partial(kernel, n_src, n_tgt, scale),
        out_shape=(
            jax.ShapeDtypeStruct((f, rows), f32),
            jax.ShapeDtypeStruct((k, rows), f32),
            jax.ShapeDtypeStruct((f, cols), f32),
            jax.ShapeDtypeStruct((k, cols), f32),
        ),
        in_specs=[pl.BlockSpec(memory_space=pl.ANY)] * 5,
        out_specs=(vmem,) * 4,
        scratch_shapes=[
            pltpu.VMEM((f, rows), bf16),
            pltpu.VMEM((k, rows), bf16),
            pltpu.VMEM((f, cols), bf16),
            pltpu.VMEM((k, cols), bf16),
            pltpu.VMEM((1, k), f32),
            pltpu.VMEM((n_tgt, stack, rows), bf16),
            pltpu.VMEM((n_src, stack, cols), bf16),
            pltpu.VMEM((stack, wide), bf16),
            pltpu.VMEM((stack, wide), bf16),
            pltpu.VMEM((f + AUG, wide), bf16),
            pltpu.VMEM((k, wide), bf16),
            pltpu.VMEM((stack, wide), f32),
            pltpu.VMEM((n_tgt, f + k, rows), f32),
            pltpu.VMEM((n_tgt, f + k, rows), f32),
            pltpu.VMEM((n_src, f + k, cols), f32),
            pltpu.VMEM((n_src, f + k, cols), f32),
            dma((5,)),
            dma((n_tgt,)),
            dma((n_tgt,)),
            dma((n_src,)),
            dma((n_src,)),
            dma((n_tgt,)),
            dma((n_tgt,)),
            dma((n_src,)),
            dma((n_src,)),
        ],
        compiler_params=pltpu.CompilerParams(
            collective_id=0, has_side_effects=True, vmem_limit_bytes=63 * 1024 * 1024
        ),
    )(src_feats, src_factor, tgt_feats, tgt_factor, rank_weight.reshape(1, k))


def solution(mesh):
    src = P(None, ("src", "tgt"))
    tgt = P(None, ("tgt", "src"))
    return jax.shard_map(
        local,
        mesh=mesh,
        in_specs=(src, src, tgt, tgt, P()),
        out_specs=(src, src, tgt, tgt),
        check_vma=False,
    )
```

time: 150 us -> 21.2 us (0.14)
  waiting for transfers between devices: 81.6 us -> 0 us
  blocking collectives: 37.5 us -> 0 us
  Pallas kernels: 0 us -> 16.9 us
  between operations: 14.1 us -> 0.66 us
  matrix products: 5.84 us -> 0 us
  other arithmetic: 5.78 us -> 0 us
    unnamed x3 -> x0, waiting for transfers between devices: 62 us -> none
    all_gather x2 -> x0, blocking collectives: 37.5 us -> none  [the longest x1 31.4 us: local(): src_whole = lax.all_gather(src_stack, 'tgt', axis=1, tiled=True)]
    reduce_scatter x1 -> x0, waiting for transfers between devices: 19.6 us -> none  [local(): lax.psum_scatter(tgt_terms, 'src', scatter_dimension=1, tiled=True)]
    pallas_call x0 -> x1, Pallas kernels: none -> 16.9 us  [local(): pl.pallas_call(functools.partial(kernel, n_src, n_tgt, scale), out_shape=...]
    dot_general x30 -> x0, matrix products: 5.84 us -> none  [the longest x5 1.76 us: tile_terms(): plan_tile = jnp.dot(src_q.T, scaled_r, preferred_element_type=jnp.float32)]
    mul x4 -> x0, other arithmetic: 3.86 us -> none  [the longest x1 1.32 us: local(): tgt_sum[:feature_count] * scale]
    slice x3 -> x0, local copies, waits for them, and re-layouts: 1.66 us -> none  [the longest x1 0.92 us: local(): src_sum[feature_count:] * scale]
    unnamed x16 -> x10, local copies, waits for them, and re-layouts: 3.01 us -> 3.24 us
  transfers between devices with their start and end apart: 2 -> 0, of which waited for: 2 -> 0; matrix products, arithmetic and copies ran while one was open for 2% -> 0% of each run, Pallas kernels for 0% -> 0%
where the time goes in v1:
time: 21.2 us; the launch traced here: 20.8 us
  Pallas kernels  16.9 us (80%)
  local copies, waits for them, and re-layouts  3.24 us (15%)
  between operations  0.66 us (3%)
    pallas_call x1, Pallas kernels, local(): pl.pallas_call(functools.partial(kernel, n_src, n_tgt, scale), out_shape=...  16.9 us
    unnamed x10, local copies, waits for them, and re-layouts  3.24 us

profile of v1, /device:TPU:0, one launch (start us, length us, event | category | flops | bytes accessed | tf_op | source)
XLA Modules:
  0.0 20.8 jit_solution(2576736421298152055)
XLA Ops:
  0.6 16.9 %shard_map.84 = (f32[32,80]{1,0:T(8,128)}, f32[16,80]{1,0:T(8,128)}, f32[32,128]{1,0:T(8,128)}, f32[16,128]{1,0:T(8,128)}) custom-call(bf16[32,80]{1,0:T(8,128)(2,1)} %x_hbm.1, bf16[16,80]{1,0:T(8,128)(2,1)} %q_hbm.1, bf16[32,128]{1,0:T(8,128)(2,1)} %y_hbm.1, bf16[16,128]{1,0:T(8,128)(2,1)} %r_hbm.1, f32[1,16]{1,0:T(1,128)} %bitcast.1), custom_call_target="tpu_custom_call" | custom-call | tf_op jit(solution)/shard_map/pallas_call | solution.py:228
  17.5 0.0 copy-start.2
  17.5 0.0 copy-start
  17.5 1.3 %copy.13 = f32[32,80]{1,0:T(8,128)} copy(f32[32,80]{1,0:T(8,128)} %get-tuple-element.8) | data formatting | bytes 20480
  18.9 0.0 copy-done.2
  18.9 0.6 %copy.14 = f32[16,80]{1,0:T(8,128)} copy(f32[16,80]{1,0:T(8,128)S(1)} %copy-done.2) | data formatting | bytes 10240
  19.5 0.0 copy-done
  19.5 0.0 copy-start.1
  19.5 0.6 %copy.15 = f32[32,128]{1,0:T(8,128)} copy(f32[32,128]{1,0:T(8,128)S(1)} %copy-done) | data formatting | bytes 32768
  20.1 0.1 copy-done.1
  20.2 0.6 %copy.16 = f32[16,128]{1,0:T(8,128)} copy(f32[16,128]{1,0:T(8,128)S(1)} %copy-done.1) | data formatting | bytes 16384
Async XLA Ops:
  17.5 1.4 %copy-start.2 = (f32[16,80]{1,0:T(8,128)S(1)}, f32[16,80]{1,0:T(8,128)}, u32[]{:S(2)}) copy-start(f32[16,80]{1,0:T(8,128)} %get-tuple-element.9) | copy-start | bytes 15364
  17.5 1.9 %copy-start = (f32[32,128]{1,0:T(8,128)S(1)}, f32[32,128]{1,0:T(8,128)}, u32[]{:S(2)}) copy-start(f32[32,128]{1,0:T(8,128)} %get-tuple-element.10) | copy-start | bytes 49156
  19.5 0.7 %copy-start.1 = (f32[16,128]{1,0:T(8,128)S(1)}, f32[16,128]{1,0:T(8,128)}, u32[]{:S(2)}) copy-start(f32[16,128]{1,0:T(8,128)} %get-tuple-element.11) | copy-start | bytes 24580

commit v2 on v1

v2 whole, which is shorter than its diff:
```python
import functools

import jax
import jax.numpy as jnp
from jax import lax
from jax.experimental import pallas as pl
from jax.experimental.pallas import tpu as pltpu
from jax.sharding import PartitionSpec as P

MESH = pl.DeviceIdType.MESH
NT = (((1,), (1,)), ((), ()))
AUG = 16


def each(low, high, body):
    if high - low <= 8:
        for i in range(low, high):
            body(i)
    else:
        lax.fori_loop(low, high, lambda i, c: (body(i), c)[1], 0)


def split3(value):
    high = value.astype(jnp.bfloat16).astype(jnp.float32)
    rest = value - high
    mid = rest.astype(jnp.bfloat16).astype(jnp.float32)
    return high, mid, rest - mid


def aug_rows(feats, first, ones_at, extra):
    norm = jnp.sum(feats * feats, axis=0, keepdims=True) + extra
    high, mid, low = split3(norm)
    shape = (AUG, feats.shape[1])
    row = lax.broadcasted_iota(jnp.int32, shape, 0)
    out = jnp.where((row >= ones_at) & (row < ones_at + 3), 1.0, 0.0)
    for k, part in enumerate((high, mid, low)):
        out = jnp.where(row == first + k, jnp.broadcast_to(part, shape), out)
    return out


def kernel(
    n_src, n_tgt, low, scale,
    x_hbm, q_hbm, y_hbm, r_hbm, g_hbm,
    gx_ref, gq_ref, gy_ref, gr_ref,
    x_in, q_in, y_in, r_in, g_in,
    a_slots, t_slots, row_stack, col_stack, row_acc,
    src_out, src_in, tgt_out, tgt_in,
    load_sem, a_send, a_recv, t_send, t_recv, so_send, so_recv, to_send, to_recv,
):
    f, rows = x_in.shape
    k = q_in.shape[0]
    head = f + AUG
    stack = head + k
    half = rows // 2
    split = a_slots.shape[1]
    n_a = n_src * low
    n_b = n_tgt // low
    me_s = lax.axis_index("src")
    me_t = lax.axis_index("tgt")
    me_b = me_t // low
    me_low = me_t % low
    me_a = me_s * low + me_low

    def a_peer(d):
        return lax.rem(me_a + d, n_a)

    def b_peer(d):
        if n_b & (n_b - 1) or not isinstance(d, int):
            return lax.rem(me_b + d, n_b)
        peer, bit = me_b, 1
        while bit <= d:
            if d & bit:
                peer = peer + bit - 2 * bit * ((peer // bit) % 2)
            bit *= 2
        return peer

    def a_device(a):
        return {"src": a // low, "tgt": me_b * low + a % low}

    def b_device(b):
        return {"src": me_s, "tgt": b * low + me_low}

    loads = [
        pltpu.make_async_copy(src, dst, load_sem.at[i])
        for i, (src, dst) in enumerate(
            ((x_hbm, x_in), (q_hbm, q_in), (y_hbm, y_in), (r_hbm, r_in), (g_hbm, g_in))
        )
    ]
    for load in loads:
        load.start()

    barrier = pltpu.get_barrier_semaphore()

    def greet(device):
        pl.semaphore_signal(barrier, inc=1, device_id=device, device_id_type=MESH)

    each(1, n_a, lambda d: greet(a_device(a_peer(d))))
    each(1, n_b, lambda d: greet(b_device(b_peer(d))))

    for load in loads:
        load.wait()

    x = x_in[...].astype(jnp.float32)
    mine = jnp.concatenate([x * -2.0, aug_rows(x, 0, 3, 0.0), q_in[...].astype(jnp.float32)], 0)
    mine = mine.T.astype(jnp.bfloat16)
    a_slots[me_a, :, 0:stack] = mine[0:split]
    a_slots[me_a, 0 : rows - split, stack : 2 * stack] = mine[split:]
    inv_row = 1.0 / g_in[...]
    square = (k, k)
    diagonal = lax.broadcasted_iota(jnp.int32, square, 0) == lax.broadcasted_iota(
        jnp.int32, square, 1
    )
    inverse_g = jnp.sum(
        jnp.where(diagonal, jnp.broadcast_to(inv_row, square), 0.0), axis=1, keepdims=True
    )
    y = y_in[...]
    t_slots[me_b, 0:f, :] = y
    t_slots[me_b, f:head, :] = aug_rows(y.astype(jnp.float32), 3, 0, 1.0).astype(jnp.bfloat16)
    t_slots[me_b, head:, :] = (r_in[...].astype(jnp.float32) * inverse_g).astype(jnp.bfloat16)

    pl.semaphore_wait(barrier, n_a + n_b - 2)

    def remote(src, dst, send, recv, device):
        return pltpu.make_async_remote_copy(
            src_ref=src, dst_ref=dst, send_sem=send, recv_sem=recv,
            device_id=device, device_id_type=MESH,
        )

    def a_copy(d, slot):
        ref = a_slots.at[slot]
        return remote(ref, ref, a_send.at[d], a_recv.at[slot], a_device(a_peer(d)))

    def t_copy(d, slot):
        ref = t_slots.at[slot]
        return remote(ref, ref, t_send.at[d], t_recv.at[slot], b_device(b_peer(d)))

    def so_copy(d, slot):
        return remote(
            src_out.at[d], src_in.at[slot], so_send.at[d], so_recv.at[slot], a_device(a_peer(d))
        )

    def to_copy(d, slot):
        return remote(
            tgt_out.at[d], tgt_in.at[slot], to_send.at[d], to_recv.at[slot], b_device(b_peer(d))
        )

    each(1, n_b, lambda d: t_copy(d, me_b).start())
    each(1, n_a, lambda d: a_copy(d, me_a).start())

    each(1, n_a, lambda d: a_copy(d, a_peer(d)).wait_recv())
    for a in range(n_a):
        row_stack[a * rows : a * rows + split, :] = a_slots[a, :, 0:stack]
        row_stack[a * rows + split : (a + 1) * rows, :] = a_slots[
            a, 0 : rows - split, stack : 2 * stack
        ]
    col_stack[...] = row_stack[...].T

    def block(d):
        first = isinstance(d, int) and d == 0
        peer = b_peer(d)
        if not first:
            t_copy(d, peer).wait_recv()
        points = t_slots[peer]
        cols = points.shape[1]
        zero_low = jnp.zeros((head, cols), jnp.bfloat16)
        zero_high = jnp.zeros((k, cols), jnp.bfloat16)
        rhs = jnp.concatenate(
            [
                jnp.concatenate([points[0:head], zero_high], 0),
                jnp.concatenate([zero_low, points[head:]], 0),
            ],
            1,
        )
        both = jnp.dot(row_stack[...], rhs, preferred_element_type=jnp.float32)
        squared, plan = both[:, 0:cols], both[:, cols:]
        inv = lax.rsqrt(squared)
        terms = jnp.concatenate(
            [(plan * inv).astype(jnp.bfloat16), (squared * inv).astype(jnp.bfloat16)], 1
        )
        col = jnp.dot(col_stack[...], terms, preferred_element_type=jnp.float32)
        mass = col[f + 3 : f + 4, 0:cols]
        tgt_out[d, 0:f, :] = points[0:f].astype(jnp.float32) * mass + 0.5 * col[0:f, 0:cols]
        tgt_out[d, f:, :] = col[head:, cols:]
        if not first:
            to_copy(d, me_b).start()
        row = lax.dot_general(terms, rhs, NT, preferred_element_type=jnp.float32)
        if first:
            row_acc[...] = row
        else:
            row_acc[...] += row

    block(0)
    each(1, n_b, block)

    def pack(d):
        start = pl.multiple_of(a_peer(d) * rows, 8)
        src_out[d, :, 0:stack] = row_acc[pl.ds(start, half), :]
        src_out[d, :, stack : 2 * stack] = row_acc[pl.ds(start + half, half), :]
        so_copy(d, me_a).start()

    each(1, n_a, pack)
    mine = pl.multiple_of(me_a * rows, 8)
    src_out[0, :, 0:stack] = row_acc[pl.ds(mine, half), :]
    src_out[0, :, stack : 2 * stack] = row_acc[pl.ds(mine + half, half), :]

    def add_tgt(d):
        peer = b_peer(d)
        to_copy(d, peer).wait_recv()
        tgt_out[0] += tgt_in[peer]

    each(1, n_b, add_tgt)
    gy_ref[...] = tgt_out[0, 0:f, :] * scale
    gr_ref[...] = tgt_out[0, f:, :] * inverse_g * scale

    def add_src(d):
        peer = a_peer(d)
        so_copy(d, peer).wait_recv()
        src_out[0] += src_in[peer]

    each(1, n_a, add_src)
    total = src_out[0]
    total = jnp.concatenate([total[:, 0:stack], total[:, stack : 2 * stack]], 0).T
    gx_ref[...] = (x * total[f : f + 1] - total[0:f]) * scale
    gq_ref[...] = total[head:] * scale

    each(1, n_a, lambda d: a_copy(d, me_a).wait_send())
    each(1, n_b, lambda d: t_copy(d, me_b).wait_send())
    each(1, n_a, lambda d: so_copy(d, me_a).wait_send())
    each(1, n_b, lambda d: to_copy(d, me_b).wait_send())


def place(*refs):
    sources, places, sems = refs[0:4], refs[4:8], refs[8]
    copies = [
        pltpu.make_async_copy(src, dst, sems.at[i])
        for i, (src, dst) in enumerate(zip(sources, places))
    ]
    for copy in copies:
        copy.start()
    for copy in copies:
        copy.wait()


def local(src_feats, src_factor, tgt_feats, tgt_factor, rank_weight):
    n_src = lax.axis_size("src")
    n_tgt = lax.axis_size("tgt")
    low = 2 if n_tgt % 2 == 0 else 1
    n_a, n_b = n_src * low, n_tgt // low
    f, rows = src_feats.shape
    k = src_factor.shape[0]
    cols = tgt_feats.shape[1]
    stack = f + AUG + k
    split = (rows // 2 + 15) // 16 * 16
    f32, bf16 = jnp.float32, jnp.bfloat16
    scale = 1.0 / (cols * n_src * n_tgt)
    vmem = pl.BlockSpec(memory_space=pltpu.VMEM)
    hbm = pl.BlockSpec(memory_space=pltpu.HBM)
    anywhere = pl.BlockSpec(memory_space=pl.ANY)
    dma = pltpu.SemaphoreType.DMA
    out_shape = (
        jax.ShapeDtypeStruct((f, rows), f32),
        jax.ShapeDtypeStruct((k, rows), f32),
        jax.ShapeDtypeStruct((f, cols), f32),
        jax.ShapeDtypeStruct((k, cols), f32),
    )
    results = pl.pallas_call(
        functools.partial(kernel, n_src, n_tgt, low, scale),
        out_shape=tuple(pltpu.VMEM(o.shape, o.dtype) for o in out_shape),
        in_specs=[hbm] * 5,
        out_specs=(vmem,) * 4,
        scratch_shapes=[
            pltpu.VMEM((f, rows), bf16),
            pltpu.VMEM((k, rows), bf16),
            pltpu.VMEM((f, cols), bf16),
            pltpu.VMEM((k, cols), bf16),
            pltpu.VMEM((1, k), f32),
            pltpu.VMEM((n_a, split, 2 * stack), bf16),
            pltpu.VMEM((n_b, stack, cols), bf16),
            pltpu.VMEM((n_a * rows, stack), bf16),
            pltpu.VMEM((stack, n_a * rows), bf16),
            pltpu.VMEM((n_a * rows, stack), f32),
            pltpu.VMEM((n_a, rows // 2, 2 * stack), f32),
            pltpu.VMEM((n_a, rows // 2, 2 * stack), f32),
            pltpu.VMEM((n_b, f + k, cols), f32),
            pltpu.VMEM((n_b, f + k, cols), f32),
            dma((5,)),
            dma((n_a,)),
            dma((n_a,)),
            dma((n_b,)),
            dma((n_b,)),
            dma((n_a,)),
            dma((n_a,)),
            dma((n_b,)),
            dma((n_b,)),
        ],
        compiler_params=pltpu.CompilerParams(
            collective_id=0, has_side_effects=True, vmem_limit_bytes=63 * 1024 * 1024
        ),
    )(src_feats, src_factor, tgt_feats, tgt_factor, rank_weight.reshape(1, k))
    return pl.pallas_call(
        place,
        out_shape=out_shape,
        in_specs=[anywhere] * 4,
        out_specs=(hbm,) * 4,
        scratch_shapes=[dma((4,))],
    )(*results)


def solution(mesh):
    src = P(None, ("src", "tgt"))
    tgt = P(None, ("tgt", "src"))
    return jax.shard_map(
        local,
        mesh=mesh,
        in_specs=(src, src, tgt, tgt, P()),
        out_specs=(src, src, tgt, tgt),
        check_vma=False,
    )
```

time: 21.2 us -> 21.8 us (1.028)
  Pallas kernels: 16.9 us -> 18.6 us
  local copies, waits for them, and re-layouts: 3.24 us -> 2.38 us
    pallas_call x1 -> x2, Pallas kernels: 16.9 us -> 18.6 us  [the longest x1 15.9 us: local(): pl.pallas_call(functools.partial(kernel, n_src, n_tgt, low, scale), out_s...]
    unnamed x10 -> x8, local copies, waits for them, and re-layouts: 3.24 us -> 2.38 us
where the time goes in v2:
time: 21.8 us; the launch traced here: 21.6 us
  Pallas kernels  18.6 us (85%)
  local copies, waits for them, and re-layouts  2.38 us (11%)
  between operations  0.65 us (3%)
    pallas_call x1, Pallas kernels, local(): pl.pallas_call(functools.partial(kernel, n_src, n_tgt, low, scale), out_s...  15.9 us
    pallas_call x1, Pallas kernels, local(): pl.pallas_call(place, out_shape=out_shape, in_specs=[anywhere] * 4, out_s...  2.62 us
    unnamed x8, local copies, waits for them, and re-layouts  2.38 us

profile of v2, /device:TPU:0, one launch (start us, length us, event | category | flops | bytes accessed | tf_op | source)
XLA Modules:
  0.0 21.6 jit_solution(5288981329689297368)
XLA Ops:
  0.6 15.9 %shard_map.84 = (f32[32,80]{1,0:T(8,128)S(1)}, f32[16,80]{1,0:T(8,128)S(1)}, f32[32,128]{1,0:T(8,128)S(1)}, f32[16,128]{1,0:T(8,128)S(1)}) custom-call(bf16[32,80]{1,0:T(8,128)(2,1)} %x_hbm.1, bf16[16,80]{1,0:T(8,128)(2,1)} %q_hbm.1, bf16[32,128]{1,0:T(8,128)(2,1)} %y_hbm.1, bf16[16,128]{1,0:T(8,128)(2,1)} %r_hbm.1, f32[1,16]{1,0:T(1,128)} %bitcast.1), custom_call_target="tpu_custom_call" | custom-call | tf_op jit(solution)/shard_map/pallas_call | solution.py:266
  16.6 0.0 copy-start
  16.6 0.6 %copy-done = f32[32,80]{1,0:T(8,128)} copy-done((f32[32,80]{1,0:T(8,128)}, f32[32,80]{1,0:T(8,128)S(1)}, u32[]{:S(2)}) %copy-start) | copy-done | bytes 10264
  17.2 0.0 copy-start.1
  17.2 0.6 %copy-done.1 = f32[32,128]{1,0:T(8,128)} copy-done((f32[32,128]{1,0:T(8,128)}, f32[32,128]{1,0:T(8,128)S(1)}, u32[]{:S(2)}) %copy-start.1) | copy-done | bytes 16408
  17.8 0.0 copy-start.2
  17.8 0.6 %copy-done.2 = f32[16,80]{1,0:T(8,128)} copy-done((f32[16,80]{1,0:T(8,128)}, f32[16,80]{1,0:T(8,128)S(1)}, u32[]{:S(2)}) %copy-start.2) | copy-done | bytes 5144
  18.4 0.0 copy-start.3
  18.4 0.6 %copy-done.3 = f32[16,128]{1,0:T(8,128)} copy-done((f32[16,128]{1,0:T(8,128)}, f32[16,128]{1,0:T(8,128)S(1)}, u32[]{:S(2)}) %copy-start.3) | copy-done | bytes 8216
  19.0 2.6 %shard_map.85 = (f32[32,80]{1,0:T(8,128)}, f32[16,80]{1,0:T(8,128)}, f32[32,128]{1,0:T(8,128)}, f32[16,128]{1,0:T(8,128)}) custom-call(f32[32,80]{1,0:T(8,128)} %copy-done, f32[16,80]{1,0:T(8,128)} %copy-done.2, f32[32,128]{1,0:T(8,128)} %copy-done.1, f32[16,128]{1,0:T(8,128)} %copy-done.3), custom_call_target="tpu_custom_call" | custom-call | tf_op jit(solution)/shard_map/pallas_call | solution.py:300
Async XLA Ops:
  16.6 0.6 %copy-start = (f32[32,80]{1,0:T(8,128)}, f32[32,80]{1,0:T(8,128)S(1)}, u32[]{:S(2)}) copy-start(f32[32,80]{1,0:T(8,128)S(1)} %get-tuple-element.8.refs_0_) | copy-start | bytes 30724
  17.2 0.6 %copy-start.1 = (f32[32,128]{1,0:T(8,128)}, f32[32,128]{1,0:T(8,128)S(1)}, u32[]{:S(2)}) copy-start(f32[32,128]{1,0:T(8,128)S(1)} %get-tuple-element.10.refs_2_) | copy-start | bytes 49156
  17.8 0.6 %copy-start.2 = (f32[16,80]{1,0:T(8,128)}, f32[16,80]{1,0:T(8,128)S(1)}, u32[]{:S(2)}) copy-start(f32[16,80]{1,0:T(8,128)S(1)} %get-tuple-element.9.refs_1_) | copy-start | bytes 15364
  18.4 0.6 %copy-start.3 = (f32[16,128]{1,0:T(8,128)}, f32[16,128]{1,0:T(8,128)S(1)}, u32[]{:S(2)}) copy-start(f32[16,128]{1,0:T(8,128)S(1)} %get-tuple-element.11.refs_3_) | copy-start | bytes 24580

commit v3 on v2

--- a/solution.py
+++ b/solution.py
@@ -18,6 +18,14 @@
             body(i)
     else:
         lax.fori_loop(low, high, lambda i, c: (body(i), c)[1], 0)
+
+
+def fold(low, high, start, body):
+    if high - low <= 8:
+        for i in range(low, high):
+            start = body(i, start)
+        return start
+    return lax.fori_loop(low, high, body, start)
 
 
 def split3(value):
@@ -126,28 +134,32 @@
             device_id=device, device_id_type=MESH,
         )
 
+    def wait_all(slots, sem):
+        ref = slots.at[pl.ds(0, slots.shape[0] - 1)]
+        pltpu.make_async_copy(ref, ref, sem.at[0]).wait()
+
     def a_copy(d, slot):
         ref = a_slots.at[slot]
-        return remote(ref, ref, a_send.at[d], a_recv.at[slot], a_device(a_peer(d)))
+        return remote(ref, ref, a_send.at[0], a_recv.at[0], a_device(a_peer(d)))
 
     def t_copy(d, slot):
         ref = t_slots.at[slot]
-        return remote(ref, ref, t_send.at[d], t_recv.at[slot], b_device(b_peer(d)))
+        return remote(ref, ref, t_send.at[0], t_recv.at[slot], b_device(b_peer(d)))
 
     def so_copy(d, slot):
         return remote(
-            src_out.at[d], src_in.at[slot], so_send.at[d], so_recv.at[slot], a_device(a_peer(d))
+            src_out.at[d], src_in.at[slot], so_send.at[0], so_recv.at[0], a_device(a_peer(d))
         )
 
     def to_copy(d, slot):
         return remote(
-            tgt_out.at[d], tgt_in.at[slot], to_send.at[d], to_recv.at[slot], b_device(b_peer(d))
+            tgt_out.at[d], tgt_in.at[slot], to_send.at[0], to_recv.at[0], b_device(b_peer(d))
         )
 
     each(1, n_b, lambda d: t_copy(d, me_b).start())
     each(1, n_a, lambda d: a_copy(d, me_a).start())
 
-    each(1, n_a, lambda d: a_copy(d, a_peer(d)).wait_recv())
+    wait_all(a_slots, a_recv)
     for a in range(n_a):
         row_stack[a * rows : a * rows + split, :] = a_slots[a, :, 0:stack]
         row_stack[a * rows + split : (a + 1) * rows, :] = a_slots[
@@ -203,30 +215,21 @@
     src_out[0, :, 0:stack] = row_acc[pl.ds(mine, half), :]
     src_out[0, :, stack : 2 * stack] = row_acc[pl.ds(mine + half, half), :]
 
-    def add_tgt(d):
-        peer = b_peer(d)
-        to_copy(d, peer).wait_recv()
-        tgt_out[0] += tgt_in[peer]
-
-    each(1, n_b, add_tgt)
-    gy_ref[...] = tgt_out[0, 0:f, :] * scale
-    gr_ref[...] = tgt_out[0, f:, :] * inverse_g * scale
-
-    def add_src(d):
-        peer = a_peer(d)
-        so_copy(d, peer).wait_recv()
-        src_out[0] += src_in[peer]
-
-    each(1, n_a, add_src)
-    total = src_out[0]
+    wait_all(tgt_in, to_recv)
+    total = fold(1, n_b, tgt_out[0], lambda d, sum_: sum_ + tgt_in[b_peer(d)])
+    gy_ref[...] = total[0:f] * scale
+    gr_ref[...] = total[f:] * inverse_g * scale
+
+    wait_all(src_in, so_recv)
+    total = fold(1, n_a, src_out[0], lambda d, sum_: sum_ + src_in[a_peer(d)])
     total = jnp.concatenate([total[:, 0:stack], total[:, stack : 2 * stack]], 0).T
     gx_ref[...] = (x * total[f : f + 1] - total[0:f]) * scale
     gq_ref[...] = total[head:] * scale
 
-    each(1, n_a, lambda d: a_copy(d, me_a).wait_send())
-    each(1, n_b, lambda d: t_copy(d, me_b).wait_send())
-    each(1, n_a, lambda d: so_copy(d, me_a).wait_send())
-    each(1, n_b, lambda d: to_copy(d, me_b).wait_send())
+    wait_all(a_slots, a_send)
+    wait_all(t_slots, t_send)
+    wait_all(src_out, so_send)
+    wait_all(tgt_out, to_send)
 
 
 def place(*refs):
@@ -255,7 +258,6 @@
     scale = 1.0 / (cols * n_src * n_tgt)
     vmem = pl.BlockSpec(memory_space=pltpu.VMEM)
     hbm = pl.BlockSpec(memory_space=pltpu.HBM)
-    anywhere = pl.BlockSpec(memory_space=pl.ANY)
     dma = pltpu.SemaphoreType.DMA
     out_shape = (
         jax.ShapeDtypeStruct((f, rows), f32),
@@ -300,10 +302,10 @@
     return pl.pallas_call(
         place,
         out_shape=out_shape,
-        in_specs=[anywhere] * 4,
+        in_specs=[vmem] * 4,
         out_specs=(hbm,) * 4,
         scratch_shapes=[dma((4,))],
-    )(*results)
+    )(*(pltpu.with_memory_space_constraint(r, pltpu.VMEM) for r in results))
 
 
 def solution(mesh):

time: 21.8 us -> 17.4 us (0.80)
  local copies, waits for them, and re-layouts: 2.38 us -> 0 us
  Pallas kernels: 18.6 us -> 16.5 us
    unnamed x8 -> x0, local copies, waits for them, and re-layouts: 2.38 us -> none
    pallas_call x1, Pallas kernels: 2.62 us -> 0.65 us  [local(): pl.pallas_call(place, out_shape=out_shape, in_specs=[vmem] * 4, out_specs...]
where the time goes in v3:
time: 17.4 us; the launch traced here: 17.2 us
  Pallas kernels  16.5 us (95%)
  between operations  0.64 us (4%)
    pallas_call x1, Pallas kernels, local(): pl.pallas_call(functools.partial(kernel, n_src, n_tgt, low, scale), out_s...  15.9 us
    pallas_call x1, Pallas kernels, local(): pl.pallas_call(place, out_shape=out_shape, in_specs=[vmem] * 4, out_specs...  0.65 us

profile of v3, /device:TPU:0, one launch (start us, length us, event | category | flops | bytes accessed | tf_op | source)
XLA Modules:
  0.0 17.2 jit_solution(16065011981743465431)
XLA Ops:
  0.6 15.9 %shard_map.84 = (f32[32,80]{1,0:T(8,128)S(1)}, f32[16,80]{1,0:T(8,128)S(1)}, f32[32,128]{1,0:T(8,128)S(1)}, f32[16,128]{1,0:T(8,128)S(1)}) custom-call(bf16[32,80]{1,0:T(8,128)(2,1)} %x_hbm.1, bf16[16,80]{1,0:T(8,128)(2,1)} %q_hbm.1, bf16[32,128]{1,0:T(8,128)(2,1)} %y_hbm.1, bf16[16,128]{1,0:T(8,128)(2,1)} %r_hbm.1, f32[1,16]{1,0:T(1,128)} %bitcast.1), custom_call_target="tpu_custom_call" | custom-call | tf_op jit(solution)/shard_map/pallas_call | solution.py:268
  16.5 0.7 %shard_map.85 = (f32[32,80]{1,0:T(8,128)}, f32[16,80]{1,0:T(8,128)}, f32[32,128]{1,0:T(8,128)}, f32[16,128]{1,0:T(8,128)}) custom-call(f32[32,80]{1,0:T(8,128)S(1)} %get-tuple-element.8.refs_0_, f32[16,80]{1,0:T(8,128)S(1)} %get-tuple-element.9.refs_1_, f32[32,128]{1,0:T(8,128)S(1)} %get-tuple-element.10.refs_2_, f32[16,128]{1,0:T(8,128)S(1)} %get-tuple-element.11.refs_3_), custom_call_target="tpu_custom_call" | custom-call | tf_op jit(solution)/shard_map/pallas_call | solution.py:302

commit v4 on v3

--- a/solution.py
+++ b/solution.py
@@ -10,6 +10,7 @@
 MESH = pl.DeviceIdType.MESH
 NT = (((1,), (1,)), ((), ()))
 AUG = 16
+CHUNK = 128
 
 
 def each(low, high, body):
@@ -156,8 +157,8 @@
             tgt_out.at[d], tgt_in.at[slot], to_send.at[0], to_recv.at[0], b_device(b_peer(d))
         )
 
+    each(1, n_a, lambda d: a_copy(d, me_a).start())
     each(1, n_b, lambda d: t_copy(d, me_b).start())
-    each(1, n_a, lambda d: a_copy(d, me_a).start())
 
     wait_all(a_slots, a_recv)
     for a in range(n_a):
@@ -183,23 +184,41 @@
             ],
             1,
         )
-        both = jnp.dot(row_stack[...], rhs, preferred_element_type=jnp.float32)
-        squared, plan = both[:, 0:cols], both[:, cols:]
-        inv = lax.rsqrt(squared)
-        terms = jnp.concatenate(
-            [(plan * inv).astype(jnp.bfloat16), (squared * inv).astype(jnp.bfloat16)], 1
-        )
-        col = jnp.dot(col_stack[...], terms, preferred_element_type=jnp.float32)
+
+        def chunk(start, size, col):
+            part = row_stack[pl.ds(start, size), :]
+            both = jnp.dot(part, rhs, preferred_element_type=jnp.float32)
+            squared, plan = both[:, 0:cols], both[:, cols:]
+            inv = lax.rsqrt(squared)
+            terms = jnp.concatenate(
+                [(plan * inv).astype(jnp.bfloat16), (squared * inv).astype(jnp.bfloat16)], 1
+            )
+            row = lax.dot_general(terms, rhs, NT, preferred_element_type=jnp.float32)
+            if first:
+                row_acc[pl.ds(start, size), :] = row
+            else:
+                row_acc[pl.ds(start, size), :] += row
+            return col + jnp.dot(
+                col_stack[:, pl.ds(start, size)], terms, preferred_element_type=jnp.float32
+            )
+
+        col = jnp.zeros((stack, 2 * cols), jnp.float32)
+        total_rows = row_stack.shape[0]
+        count = total_rows // CHUNK
+        if count <= 8:
+            for c in range(count):
+                col = chunk(c * CHUNK, CHUNK, col)
+        else:
+            col = lax.fori_loop(
+                0, count, lambda c, v: chunk(pl.multiple_of(c * CHUNK, CHUNK), CHUNK, v), col
+            )
+        if total_rows % CHUNK:
+            col = chunk(count * CHUNK, total_rows % CHUNK, col)
         mass = col[f + 3 : f + 4, 0:cols]
         tgt_out[d, 0:f, :] = points[0:f].astype(jnp.float32) * mass + 0.5 * col[0:f, 0:cols]
         tgt_out[d, f:, :] = col[head:, cols:]
         if not first:
             to_copy(d, me_b).start()
-        row = lax.dot_general(terms, rhs, NT, preferred_element_type=jnp.float32)
-        if first:
-            row_acc[...] = row
-        else:
-            row_acc[...] += row
 
     block(0)
     each(1, n_b, block)

time: 17.4 us -> 18.1 us (1.040)
  Pallas kernels: 16.5 us -> 17.2 us
    pallas_call x1, Pallas kernels: 15.9 us -> 16.6 us  [local(): pl.pallas_call(functools.partial(kernel, n_src, n_tgt, low, scale), out_s...]
where the time goes in v4:
time: 18.1 us; the launch traced here: 17.9 us
  Pallas kernels  17.2 us (95%)
  between operations  0.64 us (4%)
    pallas_call x1, Pallas kernels, local(): pl.pallas_call(functools.partial(kernel, n_src, n_tgt, low, scale), out_s...  16.6 us
    pallas_call x1, Pallas kernels, local(): pl.pallas_call(place, out_shape=out_shape, in_specs=[vmem] * 4, out_specs...  0.65 us

profile of v4, /device:TPU:0, one launch (start us, length us, event | category | flops | bytes accessed | tf_op | source)
XLA Modules:
  0.0 17.9 jit_solution(9926823806593356102)
XLA Ops:
  0.6 16.6 %shard_map.84 = (f32[32,80]{1,0:T(8,128)S(1)}, f32[16,80]{1,0:T(8,128)S(1)}, f32[32,128]{1,0:T(8,128)S(1)}, f32[16,128]{1,0:T(8,128)S(1)}) custom-call(bf16[32,80]{1,0:T(8,128)(2,1)} %x_hbm.1, bf16[16,80]{1,0:T(8,128)(2,1)} %q_hbm.1, bf16[32,128]{1,0:T(8,128)(2,1)} %y_hbm.1, bf16[16,128]{1,0:T(8,128)(2,1)} %r_hbm.1, f32[1,16]{1,0:T(1,128)} %bitcast.1), custom_call_target="tpu_custom_call" | custom-call | tf_op jit(solution)/shard_map/pallas_call | solution.py:287
  17.2 0.7 %shard_map.85 = (f32[32,80]{1,0:T(8,128)}, f32[16,80]{1,0:T(8,128)}, f32[32,128]{1,0:T(8,128)}, f32[16,128]{1,0:T(8,128)}) custom-call(f32[32,80]{1,0:T(8,128)S(1)} %get-tuple-element.8.refs_0_, f32[16,80]{1,0:T(8,128)S(1)} %get-tuple-element.9.refs_1_, f32[32,128]{1,0:T(8,128)S(1)} %get-tuple-element.10.refs_2_, f32[16,128]{1,0:T(8,128)S(1)} %get-tuple-element.11.refs_3_), custom_call_target="tpu_custom_call" | custom-call | tf_op jit(solution)/shard_map/pallas_call | solution.py:321

commit v5 on v3

--- a/solution.py
+++ b/solution.py
@@ -73,14 +73,10 @@
         return lax.rem(me_a + d, n_a)
 
     def b_peer(d):
-        if n_b & (n_b - 1) or not isinstance(d, int):
-            return lax.rem(me_b + d, n_b)
-        peer, bit = me_b, 1
-        while bit <= d:
-            if d & bit:
-                peer = peer + bit - 2 * bit * ((peer // bit) % 2)
-            bit *= 2
-        return peer
+        return lax.rem(me_b + d, n_b)
+
+    def when(condition, body):
+        pl.when(condition)(body)
 
     def a_device(a):
         return {"src": a // low, "tgt": me_b * low + a % low}
@@ -103,7 +99,8 @@
         pl.semaphore_signal(barrier, inc=1, device_id=device, device_id_type=MESH)
 
     each(1, n_a, lambda d: greet(a_device(a_peer(d))))
-    each(1, n_b, lambda d: greet(b_device(b_peer(d))))
+    top = n_b - 1
+    each(0, n_b, lambda j: when((j > me_b) | (j == me_b - 1), lambda: greet(b_device(j))))
 
     for load in loads:
         load.wait()
@@ -126,7 +123,7 @@
     t_slots[me_b, f:head, :] = aug_rows(y.astype(jnp.float32), 3, 0, 1.0).astype(jnp.bfloat16)
     t_slots[me_b, head:, :] = (r_in[...].astype(jnp.float32) * inverse_g).astype(jnp.bfloat16)
 
-    pl.semaphore_wait(barrier, n_a + n_b - 2)
+    pl.semaphore_wait(barrier, n_a - 1 + me_b + jnp.where(me_b < top, 1, 0))
 
     def remote(src, dst, send, recv, device):
         return pltpu.make_async_remote_copy(
@@ -142,22 +139,37 @@
         ref = a_slots.at[slot]
         return remote(ref, ref, a_send.at[0], a_recv.at[0], a_device(a_peer(d)))
 
-    def t_copy(d, slot):
+    def t_copy(to, slot, sem):
         ref = t_slots.at[slot]
-        return remote(ref, ref, t_send.at[0], t_recv.at[slot], b_device(b_peer(d)))
+        return remote(ref, ref, sem, t_recv.at[slot], b_device(to))
+
+    def t_down(j):
+        return t_copy(j, me_b, t_send.at[0, j])
+
+    def t_up(j):
+        return t_copy(me_b + 1, j, t_send.at[1, j])
 
     def so_copy(d, slot):
         return remote(
             src_out.at[d], src_in.at[slot], so_send.at[0], so_recv.at[0], a_device(a_peer(d))
         )
 
-    def to_copy(d, slot):
+    def to_copy(j):
         return remote(
-            tgt_out.at[d], tgt_in.at[slot], to_send.at[0], to_recv.at[0], b_device(b_peer(d))
-        )
-
-    each(1, n_b, lambda d: t_copy(d, me_b).start())
+            tgt_out.at[j], tgt_in.at[me_b], to_send.at[0], to_recv.at[0], b_device(j)
+        )
+
     each(1, n_a, lambda d: a_copy(d, me_a).start())
+    each(0, top, lambda j: when(j < me_b, lambda: t_down(j).start()))
+
+    def t_wait(j):
+        t_copy(me_b, j, t_send.at[0, j]).wait_recv()
+
+    def hand_up(j):
+        when(j < me_b, lambda: t_wait(j))
+        when((j <= me_b) & (me_b < top), lambda: t_up(j).start())
+
+    each(0, top, hand_up)
 
     wait_all(a_slots, a_recv)
     for a in range(n_a):
@@ -169,10 +181,8 @@
 
     def block(d):
         first = isinstance(d, int) and d == 0
-        peer = b_peer(d)
-        if not first:
-            t_copy(d, peer).wait_recv()
-        points = t_slots[peer]
+        when(d > me_b, lambda: t_wait(d))
+        points = t_slots[d]
         cols = points.shape[1]
         zero_low = jnp.zeros((head, cols), jnp.bfloat16)
         zero_high = jnp.zeros((k, cols), jnp.bfloat16)
@@ -193,8 +203,7 @@
         mass = col[f + 3 : f + 4, 0:cols]
         tgt_out[d, 0:f, :] = points[0:f].astype(jnp.float32) * mass + 0.5 * col[0:f, 0:cols]
         tgt_out[d, f:, :] = col[head:, cols:]
-        if not first:
-            to_copy(d, me_b).start()
+        when(d != me_b, lambda: to_copy(d).start())
         row = lax.dot_general(terms, rhs, NT, preferred_element_type=jnp.float32)
         if first:
             row_acc[...] = row
@@ -216,7 +225,7 @@
     src_out[0, :, stack : 2 * stack] = row_acc[pl.ds(mine + half, half), :]
 
     wait_all(tgt_in, to_recv)
-    total = fold(1, n_b, tgt_out[0], lambda d, sum_: sum_ + tgt_in[b_peer(d)])
+    total = fold(1, n_b, tgt_out[me_b], lambda d, sum_: sum_ + tgt_in[b_peer(d)])
     gy_ref[...] = total[0:f] * scale
     gr_ref[...] = total[f:] * inverse_g * scale
 
@@ -227,7 +236,8 @@
     gq_ref[...] = total[head:] * scale
 
     wait_all(a_slots, a_send)
-    wait_all(t_slots, t_send)
+    each(0, top, lambda j: when(j < me_b, lambda: t_down(j).wait_send()))
+    each(0, top, lambda j: when((j <= me_b) & (me_b < top), lambda: t_up(j).wait_send()))
     wait_all(src_out, so_send)
     wait_all(tgt_out, to_send)
 
@@ -288,7 +298,7 @@
             dma((5,)),
             dma((n_a,)),
             dma((n_a,)),
-            dma((n_b,)),
+            dma((2, n_b)),
             dma((n_b,)),
             dma((n_a,)),
             dma((n_a,)),

time: 17.4 us -> 19 us (1.092)
  Pallas kernels: 16.5 us -> 18.2 us
    pallas_call x1, Pallas kernels: 15.9 us -> 17.5 us  [local(): pl.pallas_call(functools.partial(kernel, n_src, n_tgt, low, scale), out_s...]
where the time goes in v5:
time: 19 us; the launch traced here: 18.8 us
  Pallas kernels  18.2 us (96%)
  between operations  0.64 us (3%)
    pallas_call x1, Pallas kernels, local(): pl.pallas_call(functools.partial(kernel, n_src, n_tgt, low, scale), out_s...  17.5 us
    pallas_call x1, Pallas kernels, local(): pl.pallas_call(place, out_shape=out_shape, in_specs=[vmem] * 4, out_specs...  0.65 us

profile of v5, /device:TPU:0, one launch (start us, length us, event | category | flops | bytes accessed | tf_op | source)
XLA Modules:
  0.0 18.8 jit_solution(8164002247385144671)
XLA Ops:
  0.6 17.5 %shard_map.84 = (f32[32,80]{1,0:T(8,128)S(1)}, f32[16,80]{1,0:T(8,128)S(1)}, f32[32,128]{1,0:T(8,128)S(1)}, f32[16,128]{1,0:T(8,128)S(1)}) custom-call(bf16[32,80]{1,0:T(8,128)(2,1)} %x_hbm.1, bf16[16,80]{1,0:T(8,128)(2,1)} %q_hbm.1, bf16[32,128]{1,0:T(8,128)(2,1)} %y_hbm.1, bf16[16,128]{1,0:T(8,128)(2,1)} %r_hbm.1, f32[1,16]{1,0:T(1,128)} %bitcast.1), custom_call_target="tpu_custom_call" | custom-call | tf_op jit(solution)/shard_map/pallas_call | solution.py:278
  18.1 0.7 %shard_map.85 = (f32[32,80]{1,0:T(8,128)}, f32[16,80]{1,0:T(8,128)}, f32[32,128]{1,0:T(8,128)}, f32[16,128]{1,0:T(8,128)}) custom-call(f32[32,80]{1,0:T(8,128)S(1)} %get-tuple-element.8.refs_0_, f32[16,80]{1,0:T(8,128)S(1)} %get-tuple-element.9.refs_1_, f32[32,128]{1,0:T(8,128)S(1)} %get-tuple-element.10.refs_2_, f32[16,128]{1,0:T(8,128)S(1)} %get-tuple-element.11.refs_3_), custom_call_target="tpu_custom_call" | custom-call | tf_op jit(solution)/shard_map/pallas_call | solution.py:312

commit v6 on v3

--- a/solution.py
+++ b/solution.py
@@ -51,7 +51,7 @@
     x_hbm, q_hbm, y_hbm, r_hbm, g_hbm,
     gx_ref, gq_ref, gy_ref, gr_ref,
     x_in, q_in, y_in, r_in, g_in,
-    a_slots, t_slots, row_stack, col_stack, row_acc,
+    a_slots, t_slots, row_stack, col_stack, row_acc, last_terms,
     src_out, src_in, tgt_out, tgt_in,
     load_sem, a_send, a_recv, t_send, t_recv, so_send, so_recv, to_send, to_recv,
 ):
@@ -73,7 +73,7 @@
         return lax.rem(me_a + d, n_a)
 
     def b_peer(d):
-        if n_b & (n_b - 1) or not isinstance(d, int):
+        if n_b & (n_b - 1) or n_b > 8:
             return lax.rem(me_b + d, n_b)
         peer, bit = me_b, 1
         while bit <= d:
@@ -146,9 +146,9 @@
         ref = t_slots.at[slot]
         return remote(ref, ref, t_send.at[0], t_recv.at[slot], b_device(b_peer(d)))
 
-    def so_copy(d, slot):
+    def so_copy(a):
         return remote(
-            src_out.at[d], src_in.at[slot], so_send.at[0], so_recv.at[0], a_device(a_peer(d))
+            src_out.at[a], src_in.at[me_a], so_send.at[0], so_recv.at[0], a_device(a)
         )
 
     def to_copy(d, slot):
@@ -156,8 +156,8 @@
             tgt_out.at[d], tgt_in.at[slot], to_send.at[0], to_recv.at[0], b_device(b_peer(d))
         )
 
+    each(1, n_a, lambda d: a_copy(d, me_a).start())
     each(1, n_b, lambda d: t_copy(d, me_b).start())
-    each(1, n_a, lambda d: a_copy(d, me_a).start())
 
     wait_all(a_slots, a_recv)
     for a in range(n_a):
@@ -167,11 +167,7 @@
         ]
     col_stack[...] = row_stack[...].T
 
-    def block(d):
-        first = isinstance(d, int) and d == 0
-        peer = b_peer(d)
-        if not first:
-            t_copy(d, peer).wait_recv()
+    def right_side(peer):
         points = t_slots[peer]
         cols = points.shape[1]
         zero_low = jnp.zeros((head, cols), jnp.bfloat16)
@@ -183,16 +179,32 @@
             ],
             1,
         )
-        both = jnp.dot(row_stack[...], rhs, preferred_element_type=jnp.float32)
+        return points, rhs
+
+    def pair_terms(points, rhs):
+        cols = rhs.shape[1] // 2
+        both = jnp.dot(points, rhs, preferred_element_type=jnp.float32)
         squared, plan = both[:, 0:cols], both[:, cols:]
         inv = lax.rsqrt(squared)
-        terms = jnp.concatenate(
+        return jnp.concatenate(
             [(plan * inv).astype(jnp.bfloat16), (squared * inv).astype(jnp.bfloat16)], 1
         )
+
+    def put_col(d, points, terms):
+        cols = points.shape[1]
         col = jnp.dot(col_stack[...], terms, preferred_element_type=jnp.float32)
         mass = col[f + 3 : f + 4, 0:cols]
         tgt_out[d, 0:f, :] = points[0:f].astype(jnp.float32) * mass + 0.5 * col[0:f, 0:cols]
         tgt_out[d, f:, :] = col[head:, cols:]
+
+    def block(d):
+        first = isinstance(d, int) and d == 0
+        peer = b_peer(d)
+        if not first:
+            t_copy(d, peer).wait_recv()
+        points, rhs = right_side(peer)
+        terms = pair_terms(row_stack[...], rhs)
+        put_col(d, points, terms)
         if not first:
             to_copy(d, me_b).start()
         row = lax.dot_general(terms, rhs, NT, preferred_element_type=jnp.float32)
@@ -202,18 +214,33 @@
             row_acc[...] += row
 
     block(0)
-    each(1, n_b, block)
-
-    def pack(d):
-        start = pl.multiple_of(a_peer(d) * rows, 8)
-        src_out[d, :, 0:stack] = row_acc[pl.ds(start, half), :]
-        src_out[d, :, stack : 2 * stack] = row_acc[pl.ds(start + half, half), :]
-        so_copy(d, me_a).start()
-
-    each(1, n_a, pack)
-    mine = pl.multiple_of(me_a * rows, 8)
-    src_out[0, :, 0:stack] = row_acc[pl.ds(mine, half), :]
-    src_out[0, :, stack : 2 * stack] = row_acc[pl.ds(mine + half, half), :]
+    each(2, n_b, lambda d: block(n_b + 1 - d))
+
+    t_copy(1, b_peer(1)).wait_recv()
+    points, rhs = right_side(b_peer(1))
+    group = 2 if n_a % 2 == 0 else 1
+    mine = me_a // group
+
+    def finish(c):
+        base = lax.rem(mine + c, n_a // group) * group
+        at = pl.ds(pl.multiple_of(base * rows, 16), group * rows)
+        terms = pair_terms(row_stack[at, :], rhs)
+        last_terms[at, :] = terms
+        row = lax.dot_general(terms, rhs, NT, preferred_element_type=jnp.float32)
+        row = row + row_acc[at, :]
+        for i in range(group):
+            a = base + i
+            src_out[a, :, 0:stack] = row[i * rows : i * rows + half]
+            src_out[a, :, stack : 2 * stack] = row[i * rows + half : (i + 1) * rows]
+
+            @pl.when(a != me_a)
+            def _():
+                so_copy(a).start()
+
+    each(1, n_a // group, finish)
+    finish(0)
+    put_col(1, points, last_terms[...])
+    to_copy(1, me_b).start()
 
     wait_all(tgt_in, to_recv)
     total = fold(1, n_b, tgt_out[0], lambda d, sum_: sum_ + tgt_in[b_peer(d)])
@@ -221,7 +248,7 @@
     gr_ref[...] = total[f:] * inverse_g * scale
 
     wait_all(src_in, so_recv)
-    total = fold(1, n_a, src_out[0], lambda d, sum_: sum_ + src_in[a_peer(d)])
+    total = fold(1, n_a, src_out[me_a], lambda d, sum_: sum_ + src_in[a_peer(d)])
     total = jnp.concatenate([total[:, 0:stack], total[:, stack : 2 * stack]], 0).T
     gx_ref[...] = (x * total[f : f + 1] - total[0:f]) * scale
     gq_ref[...] = total[head:] * scale
@@ -281,6 +308,7 @@
             pltpu.VMEM((n_a * rows, stack), bf16),
             pltpu.VMEM((stack, n_a * rows), bf16),
             pltpu.VMEM((n_a * rows, stack), f32),
+            pltpu.VMEM((n_a * rows, 2 * cols), bf16),
             pltpu.VMEM((n_a, rows // 2, 2 * stack), f32),
             pltpu.VMEM((n_a, rows // 2, 2 * stack), f32),
             pltpu.VMEM((n_b, f + k, cols), f32),

time: 17.4 us -> 17.4 us (level)
  no operation moved by 1% of the time
where the time goes in v6:
time: 17.4 us; the launch traced here: 17.2 us
  Pallas kernels  16.5 us (95%)
  between operations  0.64 us (4%)
    pallas_call x1, Pallas kernels, local(): pl.pallas_call(functools.partial(kernel, n_src, n_tgt, low, scale), out_s...  15.9 us
    pallas_call x1, Pallas kernels, local(): pl.pallas_call(place, out_shape=out_shape, in_specs=[vmem] * 4, out_specs...  0.65 us

profile of v6, /device:TPU:0, one launch (start us, length us, event | category | flops | bytes accessed | tf_op | source)
XLA Modules:
  0.0 17.2 jit_solution(9864056473186485740)
XLA Ops:
  0.6 15.9 %shard_map.84 = (f32[32,80]{1,0:T(8,128)S(1)}, f32[16,80]{1,0:T(8,128)S(1)}, f32[32,128]{1,0:T(8,128)S(1)}, f32[16,128]{1,0:T(8,128)S(1)}) custom-call(bf16[32,80]{1,0:T(8,128)(2,1)} %x_hbm.1, bf16[16,80]{1,0:T(8,128)(2,1)} %q_hbm.1, bf16[32,128]{1,0:T(8,128)(2,1)} %y_hbm.1, bf16[16,128]{1,0:T(8,128)(2,1)} %r_hbm.1, f32[1,16]{1,0:T(1,128)} %bitcast.1), custom_call_target="tpu_custom_call" | custom-call | tf_op jit(solution)/shard_map/pallas_call | solution.py:295
  16.5 0.7 %shard_map.85 = (f32[32,80]{1,0:T(8,128)}, f32[16,80]{1,0:T(8,128)}, f32[32,128]{1,0:T(8,128)}, f32[16,128]{1,0:T(8,128)}) custom-call(f32[32,80]{1,0:T(8,128)S(1)} %get-tuple-element.8.refs_0_, f32[16,80]{1,0:T(8,128)S(1)} %get-tuple-element.9.refs_1_, f32[32,128]{1,0:T(8,128)S(1)} %get-tuple-element.10.refs_2_, f32[16,128]{1,0:T(8,128)S(1)} %get-tuple-element.11.refs_3_), custom_call_target="tpu_custom_call" | custom-call | tf_op jit(solution)/shard_map/pallas_call | solution.py:330

commit v7 on v3

--- a/solution.py
+++ b/solution.py
@@ -13,18 +13,10 @@
 
 
 def each(low, high, body):
-    if high - low <= 8:
-        for i in range(low, high):
-            body(i)
-    else:
-        lax.fori_loop(low, high, lambda i, c: (body(i), c)[1], 0)
+    lax.fori_loop(low, high, lambda i, c: (body(i), c)[1], 0)
 
 
 def fold(low, high, start, body):
-    if high - low <= 8:
-        for i in range(low, high):
-            start = body(i, start)
-        return start
     return lax.fori_loop(low, high, body, start)
 
 
@@ -73,12 +65,11 @@
         return lax.rem(me_a + d, n_a)
 
     def b_peer(d):
-        if n_b & (n_b - 1) or not isinstance(d, int):
+        if n_b & (n_b - 1):
             return lax.rem(me_b + d, n_b)
-        peer, bit = me_b, 1
-        while bit <= d:
-            if d & bit:
-                peer = peer + bit - 2 * bit * ((peer // bit) % 2)
+        peer, bit = 0, 1
+        while bit < n_b:
+            peer = peer + bit * ((me_b // bit + d // bit) % 2)
             bit *= 2
         return peer
 
@@ -156,22 +147,29 @@
             tgt_out.at[d], tgt_in.at[slot], to_send.at[0], to_recv.at[0], b_device(b_peer(d))
         )
 
+    each(1, n_a, lambda d: a_copy(d, me_a).start())
     each(1, n_b, lambda d: t_copy(d, me_b).start())
-    each(1, n_a, lambda d: a_copy(d, me_a).start())
 
     wait_all(a_slots, a_recv)
-    for a in range(n_a):
-        row_stack[a * rows : a * rows + split, :] = a_slots[a, :, 0:stack]
-        row_stack[a * rows + split : (a + 1) * rows, :] = a_slots[
+    row_acc[...] = jnp.zeros_like(row_acc)
+
+    def unpack(a):
+        start = pl.multiple_of(a * rows, 16)
+        row_stack[pl.ds(start, split), :] = a_slots[a, :, 0:stack]
+        row_stack[pl.ds(start + split, rows - split), :] = a_slots[
             a, 0 : rows - split, stack : 2 * stack
         ]
+
+    each(0, n_a, unpack)
     col_stack[...] = row_stack[...].T
 
     def block(d):
-        first = isinstance(d, int) and d == 0
         peer = b_peer(d)
-        if not first:
+
+        @pl.when(d > 0)
+        def _():
             t_copy(d, peer).wait_recv()
+
         points = t_slots[peer]
         cols = points.shape[1]
         zero_low = jnp.zeros((head, cols), jnp.bfloat16)
@@ -193,16 +191,15 @@
         mass = col[f + 3 : f + 4, 0:cols]
         tgt_out[d, 0:f, :] = points[0:f].astype(jnp.float32) * mass + 0.5 * col[0:f, 0:cols]
         tgt_out[d, f:, :] = col[head:, cols:]
-        if not first:
+
+        @pl.when(d > 0)
+        def _():
             to_copy(d, me_b).start()
+
         row = lax.dot_general(terms, rhs, NT, preferred_element_type=jnp.float32)
-        if first:
-            row_acc[...] = row
-        else:
-            row_acc[...] += row
-
-    block(0)
-    each(1, n_b, block)
+        row_acc[...] += row
+
+    each(0, n_b, block)
 
     def pack(d):
         start = pl.multiple_of(a_peer(d) * rows, 8)

time: 17.4 us -> 18.3 us (1.052)
  Pallas kernels: 16.5 us -> 17.4 us
    pallas_call x1, Pallas kernels: 15.9 us -> 16.8 us  [local(): pl.pallas_call(functools.partial(kernel, n_src, n_tgt, low, scale), out_s...]
where the time goes in v7:
time: 18.3 us; the launch traced here: 18.1 us
  Pallas kernels  17.4 us (95%)
  between operations  0.64 us (3%)
    pallas_call x1, Pallas kernels, local(): pl.pallas_call(functools.partial(kernel, n_src, n_tgt, low, scale), out_s...  16.8 us
    pallas_call x1, Pallas kernels, local(): pl.pallas_call(place, out_shape=out_shape, in_specs=[vmem] * 4, out_specs...  0.65 us

profile of v7, /device:TPU:0, one launch (start us, length us, event | category | flops | bytes accessed | tf_op | source)
XLA Modules:
  0.0 18.1 jit_solution(13918742129427759084)
XLA Ops:
  0.6 16.8 %shard_map.84 = (f32[32,80]{1,0:T(8,128)S(1)}, f32[16,80]{1,0:T(8,128)S(1)}, f32[32,128]{1,0:T(8,128)S(1)}, f32[16,128]{1,0:T(8,128)S(1)}) custom-call(bf16[32,80]{1,0:T(8,128)(2,1)} %x_hbm.1, bf16[16,80]{1,0:T(8,128)(2,1)} %q_hbm.1, bf16[32,128]{1,0:T(8,128)(2,1)} %y_hbm.1, bf16[16,128]{1,0:T(8,128)(2,1)} %r_hbm.1, f32[1,16]{1,0:T(1,128)} %bitcast.1), custom_call_target="tpu_custom_call" | custom-call | tf_op jit(solution)/shard_map/pallas_call | solution.py:265
  17.4 0.7 %shard_map.85 = (f32[32,80]{1,0:T(8,128)}, f32[16,80]{1,0:T(8,128)}, f32[32,128]{1,0:T(8,128)}, f32[16,128]{1,0:T(8,128)}) custom-call(f32[32,80]{1,0:T(8,128)S(1)} %get-tuple-element.8.refs_0_, f32[16,80]{1,0:T(8,128)S(1)} %get-tuple-element.9.refs_1_, f32[32,128]{1,0:T(8,128)S(1)} %get-tuple-element.10.refs_2_, f32[16,128]{1,0:T(8,128)S(1)} %get-tuple-element.11.refs_3_), custom_call_target="tpu_custom_call" | custom-call | tf_op jit(solution)/shard_map/pallas_call | solution.py:299

commit v8 on v3

--- a/solution.py
+++ b/solution.py
@@ -26,6 +26,10 @@
             start = body(i, start)
         return start
     return lax.fori_loop(low, high, body, start)
+
+
+def add(total, part):
+    return part if total is None else total + part
 
 
 def split3(value):
@@ -73,7 +77,7 @@
         return lax.rem(me_a + d, n_a)
 
     def b_peer(d):
-        if n_b & (n_b - 1) or not isinstance(d, int):
+        if n_b & (n_b - 1) or n_b > 8:
             return lax.rem(me_b + d, n_b)
         peer, bit = me_b, 1
         while bit <= d:
@@ -156,8 +160,8 @@
             tgt_out.at[d], tgt_in.at[slot], to_send.at[0], to_recv.at[0], b_device(b_peer(d))
         )
 
+    each(1, n_a, lambda d: a_copy(d, me_a).start())
     each(1, n_b, lambda d: t_copy(d, me_b).start())
-    each(1, n_a, lambda d: a_copy(d, me_a).start())
 
     wait_all(a_slots, a_recv)
     for a in range(n_a):
@@ -167,42 +171,50 @@
         ]
     col_stack[...] = row_stack[...].T
 
-    def block(d):
-        first = isinstance(d, int) and d == 0
-        peer = b_peer(d)
-        if not first:
-            t_copy(d, peer).wait_recv()
-        points = t_slots[peer]
-        cols = points.shape[1]
+    def blocks(several):
+        parts = []
+        for d in several:
+            peer = b_peer(d)
+            if not (isinstance(d, int) and d == 0):
+                t_copy(d, peer).wait_recv()
+            parts.append(t_slots[peer])
+        cols = parts[0].shape[1]
+        wide = cols * len(parts)
         zero_low = jnp.zeros((head, cols), jnp.bfloat16)
         zero_high = jnp.zeros((k, cols), jnp.bfloat16)
         rhs = jnp.concatenate(
-            [
-                jnp.concatenate([points[0:head], zero_high], 0),
-                jnp.concatenate([zero_low, points[head:]], 0),
-            ],
+            [jnp.concatenate([p[0:head], zero_high], 0) for p in parts]
+            + [jnp.concatenate([zero_low, p[head:]], 0) for p in parts],
             1,
         )
         both = jnp.dot(row_stack[...], rhs, preferred_element_type=jnp.float32)
-        squared, plan = both[:, 0:cols], both[:, cols:]
+        squared, plan = both[:, 0:wide], both[:, wide:]
         inv = lax.rsqrt(squared)
         terms = jnp.concatenate(
             [(plan * inv).astype(jnp.bfloat16), (squared * inv).astype(jnp.bfloat16)], 1
         )
         col = jnp.dot(col_stack[...], terms, preferred_element_type=jnp.float32)
-        mass = col[f + 3 : f + 4, 0:cols]
-        tgt_out[d, 0:f, :] = points[0:f].astype(jnp.float32) * mass + 0.5 * col[0:f, 0:cols]
-        tgt_out[d, f:, :] = col[head:, cols:]
-        if not first:
-            to_copy(d, me_b).start()
-        row = lax.dot_general(terms, rhs, NT, preferred_element_type=jnp.float32)
-        if first:
-            row_acc[...] = row
-        else:
-            row_acc[...] += row
-
-    block(0)
-    each(1, n_b, block)
+        for i, d in enumerate(several):
+            at = slice(i * cols, (i + 1) * cols)
+            mass = col[f + 3 : f + 4, at]
+            tgt_out[d, 0:f, :] = parts[i][0:f].astype(jnp.float32) * mass + 0.5 * col[0:f, at]
+            tgt_out[d, f:, :] = col[head:, wide + i * cols : wide + (i + 1) * cols]
+            if not (isinstance(d, int) and d == 0):
+                to_copy(d, me_b).start()
+        return lax.dot_general(terms, rhs, NT, preferred_element_type=jnp.float32)
+
+    size = 2 if n_b % 2 == 0 else 1
+    row = fold(
+        1, n_b // size, None,
+        lambda g, sum_: add(sum_, blocks([g * size + i for i in range(size)])),
+    ) if n_b // size <= 8 else None
+    if row is None:
+        row = lax.fori_loop(
+            1, n_b // size,
+            lambda g, sum_: sum_ + blocks([g * size + i for i in range(size)]),
+            jnp.zeros_like(row_acc),
+        )
+    row_acc[...] = row + blocks(list(range(size)))
 
     def pack(d):
         start = pl.multiple_of(a_peer(d) * rows, 8)

time: 17.4 us -> 16.7 us (0.960)
  Pallas kernels: 16.5 us -> 15.9 us
    pallas_call x1, Pallas kernels: 15.9 us -> 15.2 us  [local(): pl.pallas_call(functools.partial(kernel, n_src, n_tgt, low, scale), out_s...]
where the time goes in v8:
time: 16.7 us; the launch traced here: 16.5 us
  Pallas kernels  15.9 us (95%)
  between operations  0.64 us (4%)
    pallas_call x1, Pallas kernels, local(): pl.pallas_call(functools.partial(kernel, n_src, n_tgt, low, scale), out_s...  15.2 us
    pallas_call x1, Pallas kernels, local(): pl.pallas_call(place, out_shape=out_shape, in_specs=[vmem] * 4, out_specs...  0.65 us

profile of v8, /device:TPU:0, one launch (start us, length us, event | category | flops | bytes accessed | tf_op | source)
XLA Modules:
  0.0 16.5 jit_solution(16246043269433031855)
XLA Ops:
  0.6 15.2 %shard_map.84 = (f32[32,80]{1,0:T(8,128)S(1)}, f32[16,80]{1,0:T(8,128)S(1)}, f32[32,128]{1,0:T(8,128)S(1)}, f32[16,128]{1,0:T(8,128)S(1)}) custom-call(bf16[32,80]{1,0:T(8,128)(2,1)} %x_hbm.1, bf16[16,80]{1,0:T(8,128)(2,1)} %q_hbm.1, bf16[32,128]{1,0:T(8,128)(2,1)} %y_hbm.1, bf16[16,128]{1,0:T(8,128)(2,1)} %r_hbm.1, f32[1,16]{1,0:T(1,128)} %bitcast.1), custom_call_target="tpu_custom_call" | custom-call | tf_op jit(solution)/shard_map/pallas_call | solution.py:280
  15.8 0.7 %shard_map.85 = (f32[32,80]{1,0:T(8,128)}, f32[16,80]{1,0:T(8,128)}, f32[32,128]{1,0:T(8,128)}, f32[16,128]{1,0:T(8,128)}) custom-call(f32[32,80]{1,0:T(8,128)S(1)} %get-tuple-element.8.refs_0_, f32[16,80]{1,0:T(8,128)S(1)} %get-tuple-element.9.refs_1_, f32[32,128]{1,0:T(8,128)S(1)} %get-tuple-element.10.refs_2_, f32[16,128]{1,0:T(8,128)S(1)} %get-tuple-element.11.refs_3_), custom_call_target="tpu_custom_call" | custom-call | tf_op jit(solution)/shard_map/pallas_call | solution.py:314

commit v9 on v8

--- a/solution.py
+++ b/solution.py
@@ -26,10 +26,6 @@
             start = body(i, start)
         return start
     return lax.fori_loop(low, high, body, start)
-
-
-def add(total, part):
-    return part if total is None else total + part
 
 
 def split3(value):
@@ -203,18 +199,18 @@
                 to_copy(d, me_b).start()
         return lax.dot_general(terms, rhs, NT, preferred_element_type=jnp.float32)
 
-    size = 2 if n_b % 2 == 0 else 1
-    row = fold(
-        1, n_b // size, None,
-        lambda g, sum_: add(sum_, blocks([g * size + i for i in range(size)])),
-    ) if n_b // size <= 8 else None
-    if row is None:
+    size = next(n for n in (4, 2, 1) if n_b % n == 0)
+    if n_b // size <= 8:
+        row = blocks(list(range(size)))
+        for g in range(1, n_b // size):
+            row = row + blocks([g * size + i for i in range(size)])
+    else:
         row = lax.fori_loop(
             1, n_b // size,
             lambda g, sum_: sum_ + blocks([g * size + i for i in range(size)]),
-            jnp.zeros_like(row_acc),
-        )
-    row_acc[...] = row + blocks(list(range(size)))
+            blocks(list(range(size))),
+        )
+    row_acc[...] = row
 
     def pack(d):
         start = pl.multiple_of(a_peer(d) * rows, 8)

time: 16.7 us -> 16.7 us (level)
  no operation moved by 1% of the time
where the time goes in v9:
time: 16.7 us; the launch traced here: 16.5 us
  Pallas kernels  15.8 us (95%)
  between operations  0.64 us (4%)
    pallas_call x1, Pallas kernels, local(): pl.pallas_call(functools.partial(kernel, n_src, n_tgt, low, scale), out_s...  15.2 us
    pallas_call x1, Pallas kernels, local(): pl.pallas_call(place, out_shape=out_shape, in_specs=[vmem] * 4, out_specs...  0.65 us

profile of v9, /device:TPU:0, one launch (start us, length us, event | category | flops | bytes accessed | tf_op | source)
XLA Modules:
  0.0 16.5 jit_solution(6639421771754220562)
XLA Ops:
  0.6 15.2 %shard_map.84 = (f32[32,80]{1,0:T(8,128)S(1)}, f32[16,80]{1,0:T(8,128)S(1)}, f32[32,128]{1,0:T(8,128)S(1)}, f32[16,128]{1,0:T(8,128)S(1)}) custom-call(bf16[32,80]{1,0:T(8,128)(2,1)} %x_hbm.1, bf16[16,80]{1,0:T(8,128)(2,1)} %q_hbm.1, bf16[32,128]{1,0:T(8,128)(2,1)} %y_hbm.1, bf16[16,128]{1,0:T(8,128)(2,1)} %r_hbm.1, f32[1,16]{1,0:T(1,128)} %bitcast.1), custom_call_target="tpu_custom_call" | custom-call | tf_op jit(solution)/shard_map/pallas_call | solution.py:276
  15.8 0.7 %shard_map.85 = (f32[32,80]{1,0:T(8,128)}, f32[16,80]{1,0:T(8,128)}, f32[32,128]{1,0:T(8,128)}, f32[16,128]{1,0:T(8,128)}) custom-call(f32[32,80]{1,0:T(8,128)S(1)} %get-tuple-element.8.refs_0_, f32[16,80]{1,0:T(8,128)S(1)} %get-tuple-element.9.refs_1_, f32[32,128]{1,0:T(8,128)S(1)} %get-tuple-element.10.refs_2_, f32[16,128]{1,0:T(8,128)S(1)} %get-tuple-element.11.refs_3_), custom_call_target="tpu_custom_call" | custom-call | tf_op jit(solution)/shard_map/pallas_call | solution.py:310

commit v10 on v9

--- a/solution.py
+++ b/solution.py
@@ -51,7 +51,7 @@
     x_hbm, q_hbm, y_hbm, r_hbm, g_hbm,
     gx_ref, gq_ref, gy_ref, gr_ref,
     x_in, q_in, y_in, r_in, g_in,
-    a_slots, t_slots, row_stack, col_stack, row_acc,
+    a_slots, t_slots, row_stack, col_stack, row_acc, last_terms,
     src_out, src_in, tgt_out, tgt_in,
     load_sem, a_send, a_recv, t_send, t_recv, so_send, so_recv, to_send, to_recv,
 ):
@@ -94,16 +94,16 @@
             ((x_hbm, x_in), (q_hbm, q_in), (y_hbm, y_in), (r_hbm, r_in), (g_hbm, g_in))
         )
     ]
+    barrier = pltpu.get_barrier_semaphore()
+
+    def greet(device):
+        pl.semaphore_signal(barrier, inc=1, device_id=device, device_id_type=MESH)
+
+    each(1, n_a, lambda d: greet(a_device(a_peer(d))))
+    each(1, n_b, lambda d: greet(b_device(b_peer(d))))
+
     for load in loads:
         load.start()
-
-    barrier = pltpu.get_barrier_semaphore()
-
-    def greet(device):
-        pl.semaphore_signal(barrier, inc=1, device_id=device, device_id_type=MESH)
-
-    each(1, n_a, lambda d: greet(a_device(a_peer(d))))
-    each(1, n_b, lambda d: greet(b_device(b_peer(d))))
 
     for load in loads:
         load.wait()
@@ -146,9 +146,9 @@
         ref = t_slots.at[slot]
         return remote(ref, ref, t_send.at[0], t_recv.at[slot], b_device(b_peer(d)))
 
-    def so_copy(d, slot):
+    def so_copy(a):
         return remote(
-            src_out.at[d], src_in.at[slot], so_send.at[0], so_recv.at[0], a_device(a_peer(d))
+            src_out.at[a], src_in.at[me_a], so_send.at[0], so_recv.at[0], a_device(a)
         )
 
     def to_copy(d, slot):
@@ -167,7 +167,7 @@
         ]
     col_stack[...] = row_stack[...].T
 
-    def blocks(several):
+    def right_side(several):
         parts = []
         for d in several:
             peer = b_peer(d)
@@ -175,7 +175,6 @@
                 t_copy(d, peer).wait_recv()
             parts.append(t_slots[peer])
         cols = parts[0].shape[1]
-        wide = cols * len(parts)
         zero_low = jnp.zeros((head, cols), jnp.bfloat16)
         zero_high = jnp.zeros((k, cols), jnp.bfloat16)
         rhs = jnp.concatenate(
@@ -183,13 +182,24 @@
             + [jnp.concatenate([zero_low, p[head:]], 0) for p in parts],
             1,
         )
-        both = jnp.dot(row_stack[...], rhs, preferred_element_type=jnp.float32)
+        return parts, rhs
+
+    def pair_terms(points, rhs):
+        wide = rhs.shape[1] // 2
+        both = jnp.dot(points, rhs, preferred_element_type=jnp.float32)
         squared, plan = both[:, 0:wide], both[:, wide:]
         inv = lax.rsqrt(squared)
-        terms = jnp.concatenate(
+        return jnp.concatenate(
             [(plan * inv).astype(jnp.bfloat16), (squared * inv).astype(jnp.bfloat16)], 1
         )
+
+    def row_sums(terms, rhs):
+        return lax.dot_general(terms, rhs, NT, preferred_element_type=jnp.float32)
+
+    def put_cols(several, parts, terms):
         col = jnp.dot(col_stack[...], terms, preferred_element_type=jnp.float32)
+        cols = parts[0].shape[1]
+        wide = cols * len(parts)
         for i, d in enumerate(several):
             at = slice(i * cols, (i + 1) * cols)
             mass = col[f + 3 : f + 4, at]
@@ -197,31 +207,43 @@
             tgt_out[d, f:, :] = col[head:, wide + i * cols : wide + (i + 1) * cols]
             if not (isinstance(d, int) and d == 0):
                 to_copy(d, me_b).start()
-        return lax.dot_general(terms, rhs, NT, preferred_element_type=jnp.float32)
 
     size = next(n for n in (4, 2, 1) if n_b % n == 0)
-    if n_b // size <= 8:
-        row = blocks(list(range(size)))
-        for g in range(1, n_b // size):
-            row = row + blocks([g * size + i for i in range(size)])
-    else:
-        row = lax.fori_loop(
-            1, n_b // size,
-            lambda g, sum_: sum_ + blocks([g * size + i for i in range(size)]),
-            blocks(list(range(size))),
-        )
-    row_acc[...] = row
-
-    def pack(d):
-        start = pl.multiple_of(a_peer(d) * rows, 8)
-        src_out[d, :, 0:stack] = row_acc[pl.ds(start, half), :]
-        src_out[d, :, stack : 2 * stack] = row_acc[pl.ds(start + half, half), :]
-        so_copy(d, me_a).start()
-
-    each(1, n_a, pack)
-    mine = pl.multiple_of(me_a * rows, 8)
-    src_out[0, :, 0:stack] = row_acc[pl.ds(mine, half), :]
-    src_out[0, :, stack : 2 * stack] = row_acc[pl.ds(mine + half, half), :]
+    groups = n_b // size
+
+    def earlier(g):
+        several = [g * size + i for i in range(size)]
+        parts, rhs = right_side(several)
+        terms = pair_terms(row_stack[...], rhs)
+        put_cols(several, parts, terms)
+        row_acc[...] += row_sums(terms, rhs)
+
+    if groups > 1:
+        row_acc[...] = jnp.zeros_like(row_acc)
+        each(1, groups, earlier)
+
+    several = list(range(size))
+    parts, rhs = right_side(several)
+    piece = n_a // 2 if n_a % 2 == 0 else n_a
+    pieces = n_a // piece
+    for c in reversed(range(pieces)):
+        base = lax.rem(me_a // piece + c, pieces) * piece
+        at = pl.ds(pl.multiple_of(base * rows, 16), piece * rows)
+        terms = pair_terms(row_stack[at, :], rhs)
+        last_terms[at, :] = terms
+        row = row_sums(terms, rhs)
+        if groups > 1:
+            row = row + row_acc[at, :]
+        for i in range(piece):
+            a = base + i
+            src_out[a, :, 0:stack] = row[i * rows : i * rows + half]
+            src_out[a, :, stack : 2 * stack] = row[i * rows + half : (i + 1) * rows]
+
+            @pl.when(a != me_a)
+            def _():
+                so_copy(a).start()
+
+    put_cols(several, parts, last_terms[...])
 
     wait_all(tgt_in, to_recv)
     total = fold(1, n_b, tgt_out[0], lambda d, sum_: sum_ + tgt_in[b_peer(d)])
@@ -229,7 +251,7 @@
     gr_ref[...] = total[f:] * inverse_g * scale
 
     wait_all(src_in, so_recv)
-    total = fold(1, n_a, src_out[0], lambda d, sum_: sum_ + src_in[a_peer(d)])
+    total = fold(1, n_a, src_out[me_a], lambda d, sum_: sum_ + src_in[a_peer(d)])
     total = jnp.concatenate([total[:, 0:stack], total[:, stack : 2 * stack]], 0).T
     gx_ref[...] = (x * total[f : f + 1] - total[0:f]) * scale
     gq_ref[...] = total[head:] * scale
@@ -289,6 +311,7 @@
             pltpu.VMEM((n_a * rows, stack), bf16),
             pltpu.VMEM((stack, n_a * rows), bf16),
             pltpu.VMEM((n_a * rows, stack), f32),
+            pltpu.VMEM((n_a * rows, 2 * cols * next(n for n in (4, 2, 1) if n_b % n == 0)), bf16),
             pltpu.VMEM((n_a, rows // 2, 2 * stack), f32),
             pltpu.VMEM((n_a, rows // 2, 2 * stack), f32),
             pltpu.VMEM((n_b, f + k, cols), f32),

time: 16.7 us -> 17.6 us (1.054)
  Pallas kernels: 15.8 us -> 16.7 us
    pallas_call x1, Pallas kernels: 15.2 us -> 16.1 us  [local(): pl.pallas_call(functools.partial(kernel, n_src, n_tgt, low, scale), out_s...]
where the time goes in v10:
time: 17.6 us; the launch traced here: 17.4 us
  Pallas kernels  16.7 us (95%)
  between operations  0.64 us (4%)
    pallas_call x1, Pallas kernels, local(): pl.pallas_call(functools.partial(kernel, n_src, n_tgt, low, scale), out_s...  16.1 us
    pallas_call x1, Pallas kernels, local(): pl.pallas_call(place, out_shape=out_shape, in_specs=[vmem] * 4, out_specs...  0.65 us

profile of v10, /device:TPU:0, one launch (start us, length us, event | category | flops | bytes accessed | tf_op | source)
XLA Modules:
  0.0 17.4 jit_solution(4682062498280502235)
XLA Ops:
  0.6 16.1 %shard_map.84 = (f32[32,80]{1,0:T(8,128)S(1)}, f32[16,80]{1,0:T(8,128)S(1)}, f32[32,128]{1,0:T(8,128)S(1)}, f32[16,128]{1,0:T(8,128)S(1)}) custom-call(bf16[32,80]{1,0:T(8,128)(2,1)} %x_hbm.1, bf16[16,80]{1,0:T(8,128)(2,1)} %q_hbm.1, bf16[32,128]{1,0:T(8,128)(2,1)} %y_hbm.1, bf16[16,128]{1,0:T(8,128)(2,1)} %r_hbm.1, f32[1,16]{1,0:T(1,128)} %bitcast.1), custom_call_target="tpu_custom_call" | custom-call | tf_op jit(solution)/shard_map/pallas_call | solution.py:298
  16.7 0.7 %shard_map.85 = (f32[32,80]{1,0:T(8,128)}, f32[16,80]{1,0:T(8,128)}, f32[32,128]{1,0:T(8,128)}, f32[16,128]{1,0:T(8,128)}) custom-call(f32[32,80]{1,0:T(8,128)S(1)} %get-tuple-element.8.refs_0_, f32[16,80]{1,0:T(8,128)S(1)} %get-tuple-element.9.refs_1_, f32[32,128]{1,0:T(8,128)S(1)} %get-tuple-element.10.refs_2_, f32[16,128]{1,0:T(8,128)S(1)} %get-tuple-element.11.refs_3_), custom_call_target="tpu_custom_call" | custom-call | tf_op jit(solution)/shard_map/pallas_call | solution.py:333
